TPU v7x, 768 devices: a whole 4x8x12 slice. The times are simulated.
768 devices in a mesh: wide: 64 (over y, x, core), narrow: 12 (over z).
Axes of the slice: x: 4, y: 8, z: 12, core: 2. Of those that a mesh axis runs over, the one named last changes fastest.
Arguments:
- start_field: float32 [64, 393216], P(None, ('wide', 'narrow')), may hold values from -6 to 6
- right_side: float32 [64, 393216], P(None, ('wide', 'narrow')), may hold values from -6 to 6
- element_scale: float32 [393216], P(('wide', 'narrow')), may hold values from 2 to 6
- face_scale: float32 [6, 393216], P(None, ('wide', 'narrow')), may hold values from 0.1 to 0.6
- face_nbr: int32 [6, 393216], P(None, ('wide', 'narrow')), may hold values from -1 to 767, as said below
- send_list: int32 [4, 49152], P(None, ('wide', 'narrow')), may hold values from 0 to 511, as said below
- counts: int32 [768], P(('wide', 'narrow')), may hold values from 256 to 512, as said below
- coarse_slot: int32 [393216], P(('wide', 'narrow')), may hold values from 0 to 511, as said below
- elem_block: float32 [64, 64], replicated, may hold values from -1.5 to 1.5
- smooth_block: float32 [64, 64], replicated, may hold values from -1.5 to 1.5
- face_blocks: float32 [6, 64, 64], replicated, may hold values from -0.375 to 0.375
- prolong: float32 [8, 64, 8], replicated, may hold values from -1 to 1
- coarse_scale: float32 [49152], P(('wide', 'narrow')), may hold values from 2 to 6
- coarse_face_scale: float32 [6, 49152], P(None, ('wide', 'narrow')), may hold values from 0.1 to 0.6
- coarse_nbr: int32 [6, 49152], P(None, ('wide', 'narrow')), may hold values from -1 to 127, as said below
- coarse_send: int32 [4, 12288], P(None, ('wide', 'narrow')), may hold values from 0 to 63, as said below
- coarse_block: float32 [8, 8], replicated, may hold values from -1.5 to 1.5
- coarse_smooth: float32 [8, 8], replicated, may hold values from -1.5 to 1.5
- coarse_faces: float32 [6, 8, 8], replicated, may hold values from -0.9 to 0.9
Outputs:
- smoothed_field: float32 [64, 393216], P(None, ('wide', 'narrow'))
- coarse_correction: float32 [8, 49152], P(None, ('wide', 'narrow'))
Inputs may be any that keep to these rules, and one draw needn't show every extreme that they name: `face_nbr`: -1 marks a face without neighbour; a value below 512 names a slot of the same partition; 512 + d * 64 + j names the j-th element sent by the neighbouring partition in direction d. Each partition names every value from 512 to 767 on some face. `send_list`: row d holds, for each partition, 64 distinct local slots: row 0 goes to the partition one higher on wide, row 1 one lower on wide, rows 2 and 3 likewise on narrow, cyclically. `counts`: one partition has 512 active elements and one has 256. `coarse_slot`: within each partition a permutation of 0 to 511. `coarse_nbr`: as face_nbr, with 64 coarse elements and 16 sent in each direction. `coarse_send`: as send_list, 16 distinct local coarse elements for each partition and direction.
All inputs are finite; a program needn't handle non-finite values.
Results may differ from a plain program's by a relative error of at most 0.0003.
Values sent between devices are 32-bit elements; how exact they have to be, the bound alone decides.
A program may use at most 32 MiB of HBM per device.

v0:
```python
import jax
import jax.numpy as jnp
from jax import lax
from jax.sharding import PartitionSpec as P

CS = 3


OMEGA = 0.7
COARSE_OMEGA = 0.6
HIGH = lax.Precision.HIGHEST


def passed_along(block, axis, distance):
    devices = range(lax.axis_size(axis))
    route = [((i - distance) % len(devices), i) for i in devices]
    return lax.ppermute(block, axis, route)


def product(left, right):
    return jnp.dot(left, right, preferred_element_type=jnp.float32, precision=HIGH)


def fine_ghosts(current, sends):
    pieces = []
    for direction, offset in ((0, 1), (1, -1)):
        packet = jnp.take(current, sends[direction], axis=1)
        pieces.append(passed_along(packet, "wide", offset))
    for direction, offset in ((2, 1), (3, -1)):
        packet = jnp.take(current, sends[direction], axis=1)
        pieces.append(passed_along(packet, "narrow", offset))
    return jnp.concatenate(pieces, axis=1)


def coarse_ghosts(current, sends):
    pieces = []
    for direction, offset in ((0, 1), (1, -1)):
        packet = jnp.take(current, sends[direction], axis=1)
        pieces.append(passed_along(packet, "wide", offset))
    for direction, offset in ((2, 1), (3, -1)):
        packet = jnp.take(current, sends[direction], axis=1)
        pieces.append(passed_along(packet, "narrow", offset))
    return jnp.concatenate(pieces, axis=1)


def apply_operator(current, ghosts, scale, face_scale, table, block, faces):
    extended = jnp.concatenate([current, ghosts], axis=1)
    result = scale[None, :] * product(block, current)
    for face_index in range(6):
        target = table[face_index]
        weight = jnp.where(target >= 0, face_scale[face_index], 0.0)
        gathered = jnp.take(extended, jnp.maximum(target, 0), axis=1)
        result = result + weight[None, :] * product(faces[face_index], gathered)
    return result


def smooth_step(current, residual, active, scale, block):
    return current + OMEGA * active[None, :] * product(block, residual) / scale[None, :]


def body(
    start_field,
    right_side,
    element_scale,
    face_scale,
    face_nbr,
    send_list,
    counts,
    coarse_slot,
    elem_block,
    smooth_block,
    face_blocks,
    prolong,
    coarse_scale,
    coarse_face_scale,
    coarse_nbr,
    coarse_send,
    coarse_block,
    coarse_smooth,
    coarse_faces,
):
    rows = start_field.shape[0]
    elements = start_field.shape[1]
    active = (jnp.arange(elements, dtype=jnp.int32) < counts[0]).astype(jnp.float32)
    start = start_field * active[None, :]
    source = right_side * active[None, :]

    def fine_apply(current):
        return apply_operator(
            current,
            fine_ghosts(current, send_list),
            element_scale,
            face_scale,
            face_nbr,
            elem_block,
            face_blocks,
        )

    first_residual = source - fine_apply(start)
    smoothed = smooth_step(start, first_residual, active, element_scale, smooth_block)
    fine_residual = source - fine_apply(smoothed)
    ordered = jnp.zeros_like(fine_residual).at[:, coarse_slot].set(fine_residual)
    ordered = ordered.reshape(rows, elements // 8, 8)
    coarse_rhs = jnp.einsum("kij,ick->jc", prolong, ordered, precision=HIGH)
    correction = COARSE_OMEGA * product(coarse_smooth, coarse_rhs) / coarse_scale[None, :]
    for sweep_index in range(CS - 1):
        correction = (
            correction
            + COARSE_OMEGA
            * product(
                coarse_smooth,
                coarse_rhs
                - apply_operator(
                    correction,
                    coarse_ghosts(correction, coarse_send),
                    coarse_scale,
                    coarse_face_scale,
                    coarse_nbr,
                    coarse_block,
                    coarse_faces,
                ),
            )
            / coarse_scale[None, :]
        )
    expanded = jnp.einsum("kij,jc->ick", prolong, correction, precision=HIGH).reshape(
        rows, elements
    )
    delta = active[None, :] * jnp.take(expanded, coarse_slot, axis=1)
    corrected = smoothed + delta
    final_residual = source - fine_apply(corrected)
    smoothed_field = smooth_step(corrected, final_residual, active, element_scale, smooth_block)
    return (smoothed_field, correction)


def solution(mesh):
    return jax.shard_map(
        body,
        mesh=mesh,
        in_specs=(
            P(None, ("wide", "narrow")),
            P(None, ("wide", "narrow")),
            P(("wide", "narrow")),
            P(None, ("wide", "narrow")),
            P(None, ("wide", "narrow")),
            P(None, ("wide", "narrow")),
            P(("wide", "narrow")),
            P(("wide", "narrow")),
            P(),
            P(),
            P(),
            P(),
            P(("wide", "narrow")),
            P(None, ("wide", "narrow")),
            P(None, ("wide", "narrow")),
            P(None, ("wide", "narrow")),
            P(),
            P(),
            P(),
        ),
        out_specs=(P(None, ("wide", "narrow")), P(None, ("wide", "narrow"))),
        check_vma=False,
    )
```

profile of v0, /device:TPU:1, one launch (start us, length us, event | category | flops | bytes accessed | tf_op | source)
XLA Modules:
  0.0 163.1 jit_solution(15715826294927833057)
XLA Ops:
  1.3 0.9 broadcast_multiply_fusion
  3.0 0.6 gather_fusion.2
  3.7 12.4 %collective-permute-start.1 = (f32[64,64]{1,0:T(8,128)S(1)}, f32[64,64]{1,0:T(8,128)S(1)}, u32[]{:S(2)}, u32[]{:S(2)}) collective-permute-start(f32[64,64]{1,0:T(8,128)S(1)} %select_bitcast_fusion.10), channel_id=1, source_target_pairs={{12,0},{24,12},{36,24},{48,36},{60,48},{72,60},{84,72},{96,84},{10... | collective-permute-start | bytes 49160 | tf_op jit(solution)/shard_map/ppermute | solution.py:17
  16.1 0.6 gather_fusion.3
  16.8 1.9 %collective-permute-start.2 = (f32[64,64]{1,0:T(8,128)S(1)}, f32[64,64]{1,0:T(8,128)S(1)}, u32[]{:S(2)}, u32[]{:S(2)}) collective-permute-start(f32[64,64]{1,0:T(8,128)S(1)} %select_bitcast_fusion.9), channel_id=1, source_target_pairs={{11,0},{0,1},{1,2},{2,3},{3,4},{4,5},{5,6},{6,7},{7,8},{8,9},{9,10... | collective-permute-start | bytes 49160 | tf_op jit(solution)/shard_map/ppermute | solution.py:17
  18.7 0.6 gather_fusion.4
  19.4 5.3 %collective-permute-start.3 = (f32[64,64]{1,0:T(8,128)S(1)}, f32[64,64]{1,0:T(8,128)S(1)}, u32[]{:S(2)}, u32[]{:S(2)}) collective-permute-start(f32[64,64]{1,0:T(8,128)S(1)} %select_bitcast_fusion.8), channel_id=1, source_target_pairs={{1,0},{2,1},{3,2},{4,3},{5,4},{6,5},{7,6},{8,7},{9,8},{10,9},{11,1... | collective-permute-start | bytes 49160 | tf_op jit(solution)/shard_map/ppermute | solution.py:17
  24.8 0.6 gather_fusion.1
  25.4 3.3 %collective-permute-start = (f32[64,64]{1,0:T(8,128)S(1)}, f32[64,64]{1,0:T(8,128)S(1)}, u32[]{:S(2)}, u32[]{:S(2)}) collective-permute-start(f32[64,64]{1,0:T(8,128)S(1)} %select_bitcast_fusion.11), channel_id=1, source_target_pairs={{756,0},{0,12},{12,24},{24,36},{36,48},{48,60},{60,72},{72,84},{84... | collective-permute-start | bytes 49160 | tf_op jit(solution)/shard_map/ppermute | solution.py:17
  29.0 0.6 copy-done.9
  29.7 0.7 copy-done.15
  30.4 0.7 copy-done.10
  31.1 0.7 copy-done.13
  31.9 1.6 collective-permute-done
  33.7 1.0 gather_fusion.9
  34.7 1.0 gather_fusion.8
  35.8 1.0 gather_fusion.7
  36.8 1.0 gather_fusion.6
  37.9 1.0 gather_fusion.5
  38.9 1.0 gather_fusion.10
  44.6 0.6 gather_fusion.12
  45.8 0.6 gather_fusion.14
  47.1 7.9 %collective-permute-start.5 = (f32[64,64]{1,0:T(8,128)S(1)}, f32[64,64]{1,0:T(8,128)S(1)}, u32[]{:S(2)}, u32[]{:S(2)}) collective-permute-start(f32[64,64]{1,0:T(8,128)S(1)} %select_bitcast_fusion.6), channel_id=1, source_target_pairs={{12,0},{24,12},{36,24},{48,36},{60,48},{72,60},{84,72},{96,84},{10... | collective-permute-start | bytes 49160 | tf_op jit(solution)/shard_map/ppermute | solution.py:17
  55.1 1.9 %collective-permute-start.6 = (f32[64,64]{1,0:T(8,128)S(1)}, f32[64,64]{1,0:T(8,128)S(1)}, u32[]{:S(2)}, u32[]{:S(2)}) collective-permute-start(f32[64,64]{1,0:T(8,128)S(1)} %select_bitcast_fusion.5), channel_id=1, source_target_pairs={{11,0},{0,1},{1,2},{2,3},{3,4},{4,5},{5,6},{6,7},{7,8},{8,9},{9,10... | collective-permute-start | bytes 49160 | tf_op jit(solution)/shard_map/ppermute | solution.py:17
  57.1 4.6 %collective-permute-start.7 = (f32[64,64]{1,0:T(8,128)S(1)}, f32[64,64]{1,0:T(8,128)S(1)}, u32[]{:S(2)}, u32[]{:S(2)}) collective-permute-start(f32[64,64]{1,0:T(8,128)S(1)} %select_bitcast_fusion.4), channel_id=1, source_target_pairs={{1,0},{2,1},{3,2},{4,3},{5,4},{6,5},{7,6},{8,7},{9,8},{10,9},{11,1... | collective-permute-start | bytes 49160 | tf_op jit(solution)/shard_map/ppermute | solution.py:17
  61.7 1.9 %collective-permute-start.4 = (f32[64,64]{1,0:T(8,128)S(1)}, f32[64,64]{1,0:T(8,128)S(1)}, u32[]{:S(2)}, u32[]{:S(2)}) collective-permute-start(f32[64,64]{1,0:T(8,128)S(1)} %select_bitcast_fusion.7), channel_id=1, source_target_pairs={{756,0},{0,12},{12,24},{24,36},{36,48},{48,60},{60,72},{72,84},{84... | collective-permute-start | bytes 49160 | tf_op jit(solution)/shard_map/ppermute | solution.py:17
  63.7 2.8 %collective-permute-done.4 = f32[64,64]{1,0:T(8,128)S(1)} collective-permute-done((f32[64,64]{1,0:T(8,128)S(1)}, f32[64,64]{1,0:T(8,128)S(1)}, u32[]{:S(2)}, u32[]{:S(2)}) %collective-permute-start.4) | collective-permute-done | bytes 16416 | tf_op jit(solution)/shard_map/ppermute | solution.py:17
  66.7 1.0 gather_fusion.19
  67.8 1.0 gather_fusion.18
  68.8 1.0 gather_fusion.17
  69.9 1.0 gather_fusion.16
  70.9 1.0 gather_fusion.15
  72.0 1.0 gather_fusion.20
  76.5 1.8 %scatter_custom_fusion = f32[64,512]{0,1:T(8,128)S(1)} fusion(s32[512]{0:T(512)S(1)} %compare_select_fusion.12, f32[512,64]{1,0:T(8,128)S(1)} %copy.122, f32[]{:T(128)} %constant.33.clone.1), kind=kCustom, calls=%fused_computation.203 | custom fusion | bytes 131076 | tf_op jit(solution)/shard_map/scatter | solution.py:102
  79.9 1.9 %collective-permute-start.10 = (f32[8,16]{1,0:T(8,128)S(1)}, f32[8,16]{1,0:T(8,128)S(1)}, u32[]{:S(2)}, u32[]{:S(2)}) collective-permute-start(f32[8,16]{1,0:T(8,128)S(1)} %select_bitcast_fusion.17), channel_id=1, source_target_pairs={{11,0},{0,1},{1,2},{2,3},{3,4},{4,5},{5,6},{6,7},{7,8},{8,9},{9,10... | collective-permute-start | bytes 1544 | tf_op jit(solution)/shard_map/ppermute | solution.py:17
  82.4 4.6 %collective-permute-start.11 = (f32[8,16]{1,0:T(8,128)S(1)}, f32[8,16]{1,0:T(8,128)S(1)}, u32[]{:S(2)}, u32[]{:S(2)}) collective-permute-start(f32[8,16]{1,0:T(8,128)S(1)} %select_bitcast_fusion.16), channel_id=1, source_target_pairs={{1,0},{2,1},{3,2},{4,3},{5,4},{6,5},{7,6},{8,7},{9,8},{10,9},{11,1... | collective-permute-start | bytes 1544 | tf_op jit(solution)/shard_map/ppermute | solution.py:17
  87.7 8.4 %collective-permute-start.9 = (f32[8,16]{1,0:T(8,128)S(1)}, f32[8,16]{1,0:T(8,128)S(1)}, u32[]{:S(2)}, u32[]{:S(2)}) collective-permute-start(f32[8,16]{1,0:T(8,128)S(1)} %select_bitcast_fusion.18), channel_id=1, source_target_pairs={{12,0},{24,12},{36,24},{48,36},{60,48},{72,60},{84,72},{96,84},{10... | collective-permute-start | bytes 1544 | tf_op jit(solution)/shard_map/ppermute | solution.py:17
  96.7 2.2 %collective-permute-start.8 = (f32[8,16]{1,0:T(8,128)S(1)}, f32[8,16]{1,0:T(8,128)S(1)}, u32[]{:S(2)}, u32[]{:S(2)}) collective-permute-start(f32[8,16]{1,0:T(8,128)S(1)} %select_bitcast_fusion.19), channel_id=1, source_target_pairs={{756,0},{0,12},{12,24},{24,36},{36,48},{48,60},{60,72},{72,84},{84... | collective-permute-start | bytes 1544 | tf_op jit(solution)/shard_map/ppermute | solution.py:17
  99.1 0.8 collective-permute-done.8
  100.1 0.6 gather_fusion.25
  100.7 0.6 gather_fusion.26
  101.3 0.6 gather_fusion.27
  103.1 0.6 gather_fusion.30
  107.8 7.1 %collective-permute-start.13 = (f32[8,16]{1,0:T(8,128)S(1)}, f32[8,16]{1,0:T(8,128)S(1)}, u32[]{:S(2)}, u32[]{:S(2)}) collective-permute-start(f32[8,16]{1,0:T(8,128)S(1)} %select_bitcast_fusion.14), channel_id=1, source_target_pairs={{12,0},{24,12},{36,24},{48,36},{60,48},{72,60},{84,72},{96,84},{10... | collective-permute-start | bytes 1544 | tf_op jit(solution)/shard_map/ppermute | solution.py:17
  115.0 1.9 %collective-permute-start.14 = (f32[8,16]{1,0:T(8,128)S(1)}, f32[8,16]{1,0:T(8,128)S(1)}, u32[]{:S(2)}, u32[]{:S(2)}) collective-permute-start(f32[8,16]{1,0:T(8,128)S(1)} %select_bitcast_fusion.13), channel_id=1, source_target_pairs={{11,0},{0,1},{1,2},{2,3},{3,4},{4,5},{5,6},{6,7},{7,8},{8,9},{9,10... | collective-permute-start | bytes 1544 | tf_op jit(solution)/shard_map/ppermute | solution.py:17
  117.0 4.6 %collective-permute-start.15 = (f32[8,16]{1,0:T(8,128)S(1)}, f32[8,16]{1,0:T(8,128)S(1)}, u32[]{:S(2)}, u32[]{:S(2)}) collective-permute-start(f32[8,16]{1,0:T(8,128)S(1)} %select_bitcast_fusion.12), channel_id=1, source_target_pairs={{1,0},{2,1},{3,2},{4,3},{5,4},{6,5},{7,6},{8,7},{9,8},{10,9},{11,1... | collective-permute-start | bytes 1544 | tf_op jit(solution)/shard_map/ppermute | solution.py:17
  121.7 1.9 %collective-permute-start.12 = (f32[8,16]{1,0:T(8,128)S(1)}, f32[8,16]{1,0:T(8,128)S(1)}, u32[]{:S(2)}, u32[]{:S(2)}) collective-permute-start(f32[8,16]{1,0:T(8,128)S(1)} %select_bitcast_fusion.15), channel_id=1, source_target_pairs={{756,0},{0,12},{12,24},{24,36},{36,48},{48,60},{60,72},{72,84},{84... | collective-permute-start | bytes 1544 | tf_op jit(solution)/shard_map/ppermute | solution.py:17
  123.7 1.1 collective-permute-done.12
  125.0 0.6 gather_fusion.36
  126.2 0.6 gather_fusion.37
  130.9 1.0 gather_fusion
  132.2 0.6 gather_fusion.42
  134.7 7.6 %collective-permute-start.17 = (f32[64,64]{1,0:T(8,128)S(1)}, f32[64,64]{1,0:T(8,128)S(1)}, u32[]{:S(2)}, u32[]{:S(2)}) collective-permute-start(f32[64,64]{1,0:T(8,128)S(1)} %select_bitcast_fusion.2), channel_id=1, source_target_pairs={{12,0},{24,12},{36,24},{48,36},{60,48},{72,60},{84,72},{96,84},{10... | collective-permute-start | bytes 49160 | tf_op jit(solution)/shard_map/ppermute | solution.py:17
  142.4 1.9 %collective-permute-start.18 = (f32[64,64]{1,0:T(8,128)S(1)}, f32[64,64]{1,0:T(8,128)S(1)}, u32[]{:S(2)}, u32[]{:S(2)}) collective-permute-start(f32[64,64]{1,0:T(8,128)S(1)} %select_bitcast_fusion.1), channel_id=1, source_target_pairs={{11,0},{0,1},{1,2},{2,3},{3,4},{4,5},{5,6},{6,7},{7,8},{8,9},{9,10... | collective-permute-start | bytes 49160 | tf_op jit(solution)/shard_map/ppermute | solution.py:17
  144.4 4.6 %collective-permute-start.19 = (f32[64,64]{1,0:T(8,128)S(1)}, f32[64,64]{1,0:T(8,128)S(1)}, u32[]{:S(2)}, u32[]{:S(2)}) collective-permute-start(f32[64,64]{1,0:T(8,128)S(1)} %select_bitcast_fusion), channel_id=1, source_target_pairs={{1,0},{2,1},{3,2},{4,3},{5,4},{6,5},{7,6},{8,7},{9,8},{10,9},{11,1... | collective-permute-start | bytes 49160 | tf_op jit(solution)/shard_map/ppermute | solution.py:17
  149.1 1.9 %collective-permute-start.16 = (f32[64,64]{1,0:T(8,128)S(1)}, f32[64,64]{1,0:T(8,128)S(1)}, u32[]{:S(2)}, u32[]{:S(2)}) collective-permute-start(f32[64,64]{1,0:T(8,128)S(1)} %select_bitcast_fusion.3), channel_id=1, source_target_pairs={{756,0},{0,12},{12,24},{24,36},{36,48},{48,60},{60,72},{72,84},{84... | collective-permute-start | bytes 49160 | tf_op jit(solution)/shard_map/ppermute | solution.py:17
  151.1 1.2 collective-permute-done.16
  152.5 1.0 gather_fusion.45
  153.6 1.0 gather_fusion.49
  154.6 1.0 gather_fusion.48
  155.7 1.0 gather_fusion.47
  156.7 1.0 gather_fusion.46
  157.8 1.0 gather_fusion.50
  162.2 0.9 fusion.30
  (205 shorter events, 31.8 us)
Async XLA Ops:
  0.6 42.5 %copy-start = (f32[64,64]{1,0:T(8,128)S(1)}, f32[64,64]{1,0:T(8,128)}, u32[]{:S(2)}) copy-start(f32[64,64]{1,0:T(8,128)} %param.35) | copy-start | bytes 49156
  0.6 0.7 copy-start.12
  2.3 0.7 copy-start.14
  3.7 28.2 %collective-permute-start.1 = (f32[64,64]{1,0:T(8,128)S(1)}, f32[64,64]{1,0:T(8,128)S(1)}, u32[]{:S(2)}, u32[]{:S(2)}) collective-permute-start(f32[64,64]{1,0:T(8,128)S(1)} %select_bitcast_fusion.10), channel_id=1, source_target_pairs={{12,0},{24,12},{36,24},{48,36},{60,48},{72,60},{84,72},{96,84},{10... | collective-permute-start | bytes 49160 | tf_op jit(solution)/shard_map/ppermute | solution.py:17
  16.8 15.1 %collective-permute-start.2 = (f32[64,64]{1,0:T(8,128)S(1)}, f32[64,64]{1,0:T(8,128)S(1)}, u32[]{:S(2)}, u32[]{:S(2)}) collective-permute-start(f32[64,64]{1,0:T(8,128)S(1)} %select_bitcast_fusion.9), channel_id=1, source_target_pairs={{11,0},{0,1},{1,2},{2,3},{3,4},{4,5},{5,6},{6,7},{7,8},{8,9},{9,10... | collective-permute-start | bytes 49160 | tf_op jit(solution)/shard_map/ppermute | solution.py:17
  19.4 12.4 %collective-permute-start.3 = (f32[64,64]{1,0:T(8,128)S(1)}, f32[64,64]{1,0:T(8,128)S(1)}, u32[]{:S(2)}, u32[]{:S(2)}) collective-permute-start(f32[64,64]{1,0:T(8,128)S(1)} %select_bitcast_fusion.8), channel_id=1, source_target_pairs={{1,0},{2,1},{3,2},{4,3},{5,4},{6,5},{7,6},{8,7},{9,8},{10,9},{11,1... | collective-permute-start | bytes 49160 | tf_op jit(solution)/shard_map/ppermute | solution.py:17
  25.4 3.3 %copy-start.4 = (s32[6,512]{1,0:T(8,128)S(1)}, s32[6,512]{1,0:T(8,128)}, u32[]{:S(2)}) copy-start(s32[6,512]{1,0:T(8,128)} %param.31) | copy-start | bytes 36868
  25.4 8.0 %collective-permute-start = (f32[64,64]{1,0:T(8,128)S(1)}, f32[64,64]{1,0:T(8,128)S(1)}, u32[]{:S(2)}, u32[]{:S(2)}) collective-permute-start(f32[64,64]{1,0:T(8,128)S(1)} %select_bitcast_fusion.11), channel_id=1, source_target_pairs={{756,0},{0,12},{12,24},{24,36},{36,48},{48,60},{60,72},{72,84},{84... | collective-permute-start | bytes 49160 | tf_op jit(solution)/shard_map/ppermute | solution.py:17
  28.9 0.7 copy-start.9
  29.7 0.7 copy-start.15
  30.4 0.7 copy-start.10
  31.1 0.7 copy-start.13
  38.9 1.1 copy-start.1
  42.5 0.9 copy-start.2
  42.6 0.9 copy-start.5
  43.5 0.8 copy-start.16
  47.1 16.6 %collective-permute-start.5 = (f32[64,64]{1,0:T(8,128)S(1)}, f32[64,64]{1,0:T(8,128)S(1)}, u32[]{:S(2)}, u32[]{:S(2)}) collective-permute-start(f32[64,64]{1,0:T(8,128)S(1)} %select_bitcast_fusion.6), channel_id=1, source_target_pairs={{12,0},{24,12},{36,24},{48,36},{60,48},{72,60},{84,72},{96,84},{10... | collective-permute-start | bytes 49160 | tf_op jit(solution)/shard_map/ppermute | solution.py:17
  55.1 8.6 %collective-permute-start.6 = (f32[64,64]{1,0:T(8,128)S(1)}, f32[64,64]{1,0:T(8,128)S(1)}, u32[]{:S(2)}, u32[]{:S(2)}) collective-permute-start(f32[64,64]{1,0:T(8,128)S(1)} %select_bitcast_fusion.5), channel_id=1, source_target_pairs={{11,0},{0,1},{1,2},{2,3},{3,4},{4,5},{5,6},{6,7},{7,8},{8,9},{9,10... | collective-permute-start | bytes 49160 | tf_op jit(solution)/shard_map/ppermute | solution.py:17
  57.1 6.6 %collective-permute-start.7 = (f32[64,64]{1,0:T(8,128)S(1)}, f32[64,64]{1,0:T(8,128)S(1)}, u32[]{:S(2)}, u32[]{:S(2)}) collective-permute-start(f32[64,64]{1,0:T(8,128)S(1)} %select_bitcast_fusion.4), channel_id=1, source_target_pairs={{1,0},{2,1},{3,2},{4,3},{5,4},{6,5},{7,6},{8,7},{9,8},{10,9},{11,1... | collective-permute-start | bytes 49160 | tf_op jit(solution)/shard_map/ppermute | solution.py:17
  61.7 4.7 %collective-permute-start.4 = (f32[64,64]{1,0:T(8,128)S(1)}, f32[64,64]{1,0:T(8,128)S(1)}, u32[]{:S(2)}, u32[]{:S(2)}) collective-permute-start(f32[64,64]{1,0:T(8,128)S(1)} %select_bitcast_fusion.7), channel_id=1, source_target_pairs={{756,0},{0,12},{12,24},{24,36},{36,48},{48,60},{60,72},{72,84},{84... | collective-permute-start | bytes 49160 | tf_op jit(solution)/shard_map/ppermute | solution.py:17
  76.5 1.8 %copy-start.3 = (f32[8,64,8]{1,2,0:T(8,128)S(1)}, f32[8,64,8]{1,2,0:T(8,128)}, u32[]{:S(2)}) copy-start(f32[8,64,8]{1,2,0:T(8,128)} %param.38) | copy-start | bytes 49156
  78.3 0.7 copy-start.8
  78.3 0.7 copy-start.11
  79.9 19.2 %collective-permute-start.10 = (f32[8,16]{1,0:T(8,128)S(1)}, f32[8,16]{1,0:T(8,128)S(1)}, u32[]{:S(2)}, u32[]{:S(2)}) collective-permute-start(f32[8,16]{1,0:T(8,128)S(1)} %select_bitcast_fusion.17), channel_id=1, source_target_pairs={{11,0},{0,1},{1,2},{2,3},{3,4},{4,5},{5,6},{6,7},{7,8},{8,9},{9,10... | collective-permute-start | bytes 1544 | tf_op jit(solution)/shard_map/ppermute | solution.py:17
  82.4 16.6 %collective-permute-start.11 = (f32[8,16]{1,0:T(8,128)S(1)}, f32[8,16]{1,0:T(8,128)S(1)}, u32[]{:S(2)}, u32[]{:S(2)}) collective-permute-start(f32[8,16]{1,0:T(8,128)S(1)} %select_bitcast_fusion.16), channel_id=1, source_target_pairs={{1,0},{2,1},{3,2},{4,3},{5,4},{6,5},{7,6},{8,7},{9,8},{10,9},{11,1... | collective-permute-start | bytes 1544 | tf_op jit(solution)/shard_map/ppermute | solution.py:17
  87.7 11.4 %collective-permute-start.9 = (f32[8,16]{1,0:T(8,128)S(1)}, f32[8,16]{1,0:T(8,128)S(1)}, u32[]{:S(2)}, u32[]{:S(2)}) collective-permute-start(f32[8,16]{1,0:T(8,128)S(1)} %select_bitcast_fusion.18), channel_id=1, source_target_pairs={{12,0},{24,12},{36,24},{48,36},{60,48},{72,60},{84,72},{96,84},{10... | collective-permute-start | bytes 1544 | tf_op jit(solution)/shard_map/ppermute | solution.py:17
  96.7 2.2 %copy-start.7 = (f32[8,8]{1,0:T(8,128)S(1)}, f32[8,8]{1,0:T(8,128)}, u32[]{:S(2)}) copy-start(f32[8,8]{1,0:T(8,128)} %param.43) | copy-start | bytes 772
  96.7 3.2 %collective-permute-start.8 = (f32[8,16]{1,0:T(8,128)S(1)}, f32[8,16]{1,0:T(8,128)S(1)}, u32[]{:S(2)}, u32[]{:S(2)}) collective-permute-start(f32[8,16]{1,0:T(8,128)S(1)} %select_bitcast_fusion.19), channel_id=1, source_target_pairs={{756,0},{0,12},{12,24},{24,36},{36,48},{48,60},{60,72},{72,84},{84... | collective-permute-start | bytes 1544 | tf_op jit(solution)/shard_map/ppermute | solution.py:17
  103.1 0.7 copy-start.17
  107.8 15.9 %collective-permute-start.13 = (f32[8,16]{1,0:T(8,128)S(1)}, f32[8,16]{1,0:T(8,128)S(1)}, u32[]{:S(2)}, u32[]{:S(2)}) collective-permute-start(f32[8,16]{1,0:T(8,128)S(1)} %select_bitcast_fusion.14), channel_id=1, source_target_pairs={{12,0},{24,12},{36,24},{48,36},{60,48},{72,60},{84,72},{96,84},{10... | collective-permute-start | bytes 1544 | tf_op jit(solution)/shard_map/ppermute | solution.py:17
  115.0 8.7 %collective-permute-start.14 = (f32[8,16]{1,0:T(8,128)S(1)}, f32[8,16]{1,0:T(8,128)S(1)}, u32[]{:S(2)}, u32[]{:S(2)}) collective-permute-start(f32[8,16]{1,0:T(8,128)S(1)} %select_bitcast_fusion.13), channel_id=1, source_target_pairs={{11,0},{0,1},{1,2},{2,3},{3,4},{4,5},{5,6},{6,7},{7,8},{8,9},{9,10... | collective-permute-start | bytes 1544 | tf_op jit(solution)/shard_map/ppermute | solution.py:17
  117.0 6.7 %collective-permute-start.15 = (f32[8,16]{1,0:T(8,128)S(1)}, f32[8,16]{1,0:T(8,128)S(1)}, u32[]{:S(2)}, u32[]{:S(2)}) collective-permute-start(f32[8,16]{1,0:T(8,128)S(1)} %select_bitcast_fusion.12), channel_id=1, source_target_pairs={{1,0},{2,1},{3,2},{4,3},{5,4},{6,5},{7,6},{8,7},{9,8},{10,9},{11,1... | collective-permute-start | bytes 1544 | tf_op jit(solution)/shard_map/ppermute | solution.py:17
  121.7 3.1 %collective-permute-start.12 = (f32[8,16]{1,0:T(8,128)S(1)}, f32[8,16]{1,0:T(8,128)S(1)}, u32[]{:S(2)}, u32[]{:S(2)}) collective-permute-start(f32[8,16]{1,0:T(8,128)S(1)} %select_bitcast_fusion.15), channel_id=1, source_target_pairs={{756,0},{0,12},{12,24},{24,36},{36,48},{48,60},{60,72},{72,84},{84... | collective-permute-start | bytes 1544 | tf_op jit(solution)/shard_map/ppermute | solution.py:17
  130.2 0.6 copy-start.6
  134.7 16.3 %collective-permute-start.17 = (f32[64,64]{1,0:T(8,128)S(1)}, f32[64,64]{1,0:T(8,128)S(1)}, u32[]{:S(2)}, u32[]{:S(2)}) collective-permute-start(f32[64,64]{1,0:T(8,128)S(1)} %select_bitcast_fusion.2), channel_id=1, source_target_pairs={{12,0},{24,12},{36,24},{48,36},{60,48},{72,60},{84,72},{96,84},{10... | collective-permute-start | bytes 49160 | tf_op jit(solution)/shard_map/ppermute | solution.py:17
  142.4 8.6 %collective-permute-start.18 = (f32[64,64]{1,0:T(8,128)S(1)}, f32[64,64]{1,0:T(8,128)S(1)}, u32[]{:S(2)}, u32[]{:S(2)}) collective-permute-start(f32[64,64]{1,0:T(8,128)S(1)} %select_bitcast_fusion.1), channel_id=1, source_target_pairs={{11,0},{0,1},{1,2},{2,3},{3,4},{4,5},{5,6},{6,7},{7,8},{8,9},{9,10... | collective-permute-start | bytes 49160 | tf_op jit(solution)/shard_map/ppermute | solution.py:17
  144.4 6.6 %collective-permute-start.19 = (f32[64,64]{1,0:T(8,128)S(1)}, f32[64,64]{1,0:T(8,128)S(1)}, u32[]{:S(2)}, u32[]{:S(2)}) collective-permute-start(f32[64,64]{1,0:T(8,128)S(1)} %select_bitcast_fusion), channel_id=1, source_target_pairs={{1,0},{2,1},{3,2},{4,3},{5,4},{6,5},{7,6},{8,7},{9,8},{10,9},{11,1... | collective-permute-start | bytes 49160 | tf_op jit(solution)/shard_map/ppermute | solution.py:17
  149.1 3.2 %collective-permute-start.16 = (f32[64,64]{1,0:T(8,128)S(1)}, f32[64,64]{1,0:T(8,128)S(1)}, u32[]{:S(2)}, u32[]{:S(2)}) collective-permute-start(f32[64,64]{1,0:T(8,128)S(1)} %select_bitcast_fusion.3), channel_id=1, source_target_pairs={{756,0},{0,12},{12,24},{24,36},{36,48},{48,60},{60,72},{72,84},{84... | collective-permute-start | bytes 49160 | tf_op jit(solution)/shard_map/ppermute | solution.py:17
where the time goes:
time: 166 us; the launch traced here: 163 us
  starting transfers between devices  87.8 us (53%)
  local copies, waits for them, and re-layouts  48.6 us (29%)
  matrix products  15.5 us (9%)
  waiting for transfers between devices  7.41 us (4%)
  between operations  2.5 us (2%)
    ppermute x20, starting transfers between devices, passed_along(): return lax.ppermute(block, axis, route)  87.8 us
    gather x30, local copies, waits for them, and re-layouts, apply_operator(): gathered = jnp.take(extended, jnp.maximum(target, 0), axis=1)  25.8 us
    dot_general x40, matrix products, product(): jnp.dot(left, right, preferred_element_type=jnp.float32, precision=HIGH)  14.8 us
    gather x24, local copies, waits for them, and re-layouts, fine_ghosts(): packet = jnp.take(current, sends[direction], axis=1)  8.06 us
    ppermute x20, waiting for transfers between devices, passed_along(): return lax.ppermute(block, axis, route)  7.41 us
    gather x16, local copies, waits for them, and re-layouts, coarse_ghosts(): packet = jnp.take(current, sends[direction], axis=1)  5.07 us
    unnamed x36, local copies, waits for them, and re-layouts  4.73 us
  transfers between devices with their start and end apart: 20, of which 5 were waited for; matrix products, arithmetic and copies ran while one was open for 3% of the time, Pallas kernels for 0%

commit v1 on v0

v1 whole, which is shorter than its diff:
```python
import functools

import jax
import jax.numpy as jnp
from jax import lax
from jax.experimental import pallas as pl
from jax.experimental.pallas import tpu as pltpu
from jax.sharding import PartitionSpec as P

OMEGA = 0.7
COARSE_OMEGA = 0.6
HIGH = lax.Precision.HIGHEST
F32 = jnp.float32
BF16 = jnp.bfloat16
FACES = 6
GROUPS = 4
NT = (((1,), (1,)), ((), ()))


def take(values, lanes):
    return jnp.take_along_axis(values, lanes, axis=1, mode="promise_in_bounds")


def halves(x):
    high = x.astype(BF16).astype(F32)
    return high, x - high


def exact_dot(a, b):
    return jnp.dot(a, b, preferred_element_type=F32, precision=HIGH)


def stack_left(a):
    high, low = halves(a)
    return jnp.concatenate([high, low, high], axis=1).astype(BF16)


def stack_right(b):
    high, low = halves(b)
    high = high.astype(BF16)
    return jnp.concatenate([high, high, low.astype(BF16)], axis=0)


def bf_dot(a, b):
    return jnp.dot(a, b, preferred_element_type=F32)


def kernel(
    wide,
    narrow,
    start_ref,
    right_ref,
    scale_ref,
    face_scale_ref,
    nbr_ref,
    send_ref,
    counts_ref,
    slot_ref,
    elem_ref,
    smooth_ref,
    faces_ref,
    prolong_ref,
    cscale_ref,
    cface_scale_ref,
    cnbr_ref,
    csend_ref,
    cblock_ref,
    csmooth_ref,
    cfaces_ref,
    out_ref,
    corr_ref,
    x_ref,
    sm_ref,
    n_ref,
    y_ref,
    lhs_s,
    lhs_p,
    lhs_sp,
    comp_s,
    comp_p,
    final_ref,
    d_hi,
    d_lo,
    base_ref,
    t_ref,
    coef_ref,
    onehot_ref,
    codes_ref,
    pack1,
    ghost1,
    pack2,
    ghost2,
    q3,
    r3,
    q4,
    r4,
    q5,
    r5,
    send_sem,
    recv_sem,
):
    me_w = lax.axis_index("wide")
    me_n = lax.axis_index("narrow")
    targets = (
        {"wide": lax.rem(me_w + 1, wide), "narrow": me_n},
        {"wide": lax.rem(me_w + wide - 1, wide), "narrow": me_n},
        {"wide": me_w, "narrow": lax.rem(me_n + 1, narrow)},
        {"wide": me_w, "narrow": lax.rem(me_n + narrow - 1, narrow)},
    )
    barrier = pltpu.get_barrier_semaphore()
    for target in targets:
        pl.semaphore_signal(
            barrier, inc=1, device_id=target, device_id_type=pl.DeviceIdType.MESH
        )

    lane = lax.broadcasted_iota(jnp.int32, (8, 128), 1)
    lane1 = lax.broadcasted_iota(jnp.int32, (1, 128), 1)
    low32 = jnp.broadcast_to(lane1 < 64, (32, 128))
    element = lax.broadcasted_iota(jnp.int32, (1, 512), 1)
    active = jnp.where(element < counts_ref[0], 1.0, 0.0).astype(F32)

    def copies(step, sources, buffers):
        return [
            pltpu.make_async_remote_copy(
                src_ref=sources[d],
                dst_ref=buffers.at[d],
                send_sem=send_sem.at[step, d],
                recv_sem=recv_sem.at[step, d],
                device_id=targets[d],
                device_id_type=pl.DeviceIdType.MESH,
            )
            for d in range(4)
        ]

    def start_all(group):
        for d in (2, 3, 0, 1):
            group[d].start()

    def pack(field_ref, packets, codes=None):
        for pair in range(2):
            row = jnp.concatenate(
                [send_ref[2 * pair : 2 * pair + 1, :], send_ref[2 * pair + 1 : 2 * pair + 2, :]],
                axis=1,
            )
            index = jnp.broadcast_to(row & 127, (64, 128))
            group = jnp.broadcast_to(row >> 7, (64, 128))
            picked = jnp.zeros((64, 128), F32)
            for s in range(GROUPS):
                got = take(field_ref[:, s * 128 : (s + 1) * 128], index)
                picked = jnp.where(group == s, got, picked)
            moved = pltpu.roll(picked[32:], 64, 1)
            packets[2 * pair, 0:32, :] = jnp.where(low32, picked[:32], moved)
            packets[2 * pair + 1, 0:32, :] = jnp.where(low32, moved, picked[:32])
            if codes is not None:
                picked = jnp.zeros((8, 128), F32)
                for s in range(GROUPS):
                    got = take(
                        jnp.broadcast_to(codes[:, s * 128 : (s + 1) * 128], (8, 128)),
                        index[:8],
                    )
                    picked = jnp.where(group[:8] == s, got, picked)
                packets[2 * pair, 32:40, :] = picked
                packets[2 * pair + 1, 32:40, :] = picked

    def unpack(ghosts):
        columns = []
        for pair in range(2):
            a = ghosts[2 * pair, 0:32, :]
            b = ghosts[2 * pair + 1, 0:32, :]
            first = jnp.where(low32, a, b)
            second = pltpu.roll(jnp.where(low32, b, a), 64, 1)
            columns.append(jnp.concatenate([first, second], axis=0))
        return jnp.concatenate(columns, axis=1)

    def gather_faces(groups, fresh):
        for t in range(GROUPS):
            span = slice(t * 128, (t + 1) * 128)
            total = jnp.zeros((64, 128), F32) if fresh else n_ref[:, span]
            for f in range(FACES):
                row = nbr_ref[f : f + 1, span]
                index = jnp.broadcast_to(row & 127, (64, 128))
                group = jnp.broadcast_to(row >> 7, (64, 128))
                picked = jnp.zeros((64, 128), F32)
                for s in groups:
                    got = take(
                        y_ref[(f + 1) * 64 : (f + 2) * 64, s * 128 : (s + 1) * 128], index
                    )
                    picked = jnp.where(group == s, got, picked)
                total = total + face_scale_ref[f : f + 1, span] * picked
            n_ref[:, span] = total

    x_ref[...] = start_ref[...] * active
    codes = jnp.where(active > 0.0, slot_ref[...].astype(F32), -1.0)
    pack(x_ref, pack1, codes)
    pl.semaphore_wait(barrier, 4)
    first = copies(0, [pack1.at[d] for d in range(4)], ghost1)
    start_all(first)

    smooth = smooth_ref[...]
    csmooth = csmooth_ref[...]
    prolong_t = prolong_ref[...]
    for f in range(FACES + 1):
        block = elem_ref[...] if f == 0 else faces_ref[f - 1]
        comp_s[f * 64 : (f + 1) * 64, :] = exact_dot(smooth, block)
    lhs_s[...] = stack_left(comp_s[...])
    y_ref[:, :512] = bf_dot(lhs_s[...], stack_right(x_ref[...]))
    gather_faces(range(GROUPS), True)
    row_blocks = lax.broadcasted_iota(jnp.int32, (64, 64), 0) >> 3
    column_blocks = lax.broadcasted_iota(jnp.int32, (64, 64), 1) >> 3
    tiled = jnp.concatenate([csmooth] * 8, axis=1)
    tiled = jnp.concatenate([tiled] * 8, axis=0)
    diagonal = jnp.where(row_blocks == column_blocks, tiled, 0.0)
    restrict = exact_dot(diagonal, prolong_t)
    lhs_sp[...] = stack_left(jnp.concatenate([smooth, restrict], axis=0))
    t_ref[...] = bf_dot(lhs_sp[...], stack_right(right_ref[...]))
    inverse = 1.0 / scale_ref[...]
    omega = OMEGA * active

    for copy in first:
        copy.wait_recv()
    y_ref[64:, 512:] = bf_dot(lhs_s[64:, :], stack_right(unpack(ghost1)))
    gather_faces((4, 5), False)
    sm_ref[:, :512] = x_ref[...] + omega * ((t_ref[:64] - n_ref[...]) * inverse - y_ref[:64, :512])
    pack(sm_ref, pack2)
    second = copies(1, [pack2.at[d] for d in range(4)], ghost2)
    start_all(second)

    for f in range(FACES + 1):
        block = elem_ref[...] if f == 0 else faces_ref[f - 1]
        comp_p[f * 64 : (f + 1) * 64, :] = exact_dot(restrict, block)
    lhs_p[...] = stack_left(comp_p[...])
    y_ref[:, :512] = bf_dot(lhs_p[...], stack_right(sm_ref[:, :512]))
    gather_faces(range(GROUPS), True)
    n_ref[...] = active * t_ref[64:] - scale_ref[...] * y_ref[:64, :512] - n_ref[...]
    together = jnp.concatenate([cblock_ref[...]] + [cfaces_ref[f] for f in range(FACES)], axis=1)
    coarse = exact_dot(csmooth, together)
    for c in range(8 * (FACES + 1)):
        coef_ref[c] = jnp.broadcast_to(coarse[:, c : c + 1], (8, 128))
    parent = slot_ref[...] >> 3
    child = slot_ref[...] & 7
    row128 = lax.broadcasted_iota(jnp.int32, (128, 512), 0) & 63
    onehot_ref[...] = jnp.where(row128 == parent, 1.0, 0.0).astype(BF16)
    cinv = COARSE_OMEGA / jnp.concatenate([cscale_ref[...]] * 2, axis=1)
    cnbr = jnp.concatenate([cnbr_ref[...]] * 2, axis=1)
    cweight = jnp.concatenate([cface_scale_ref[...]] * 2, axis=1)
    cweight = jnp.where(cnbr >= 0, cweight, 0.0) * cinv
    clane = jnp.maximum(cnbr, 0)
    csend = csend_ref[...]
    row = jnp.concatenate([csend[d : d + 1] for d in range(4)] * 2, axis=1)
    qlane = jnp.broadcast_to(row, (8, 128))

    for copy in second:
        copy.wait_recv()
    sm_ref[:, 512:] = unpack(ghost2)
    y_ref[64:, 512:] = bf_dot(lhs_p[64:, :], stack_right(sm_ref[:, 512:]))

    def minus_faces():
        for t in range(GROUPS):
            span = slice(t * 128, (t + 1) * 128)
            total = n_ref[:, span]
            for f in range(FACES):
                row = nbr_ref[f : f + 1, span]
                index = jnp.broadcast_to(row & 127, (64, 128))
                group = jnp.broadcast_to(row >> 7, (64, 128))
                picked = jnp.zeros((64, 128), F32)
                for s in (4, 5):
                    got = take(
                        y_ref[(f + 1) * 64 : (f + 2) * 64, s * 128 : (s + 1) * 128], index
                    )
                    picked = jnp.where(group == s, got, picked)
                total = total - face_scale_ref[f : f + 1, span] * picked
            n_ref[:, span] = total

    minus_faces()
    chosen = jnp.zeros((8, 512), F32)
    for k in range(8):
        chosen = jnp.where(child == k, n_ref[8 * k : 8 * k + 8, :], chosen)
    high, low = halves(chosen)
    both = jnp.concatenate([high, low], axis=0).astype(BF16)
    summed = lax.dot_general(both, onehot_ref[...], NT, preferred_element_type=F32)
    base_c = (summed[:8] + summed[8:]) * cinv

    def extend(own, received):
        ext = own
        for d in range(4):
            here = (lane >= 64 + 16 * d) & (lane < 80 + 16 * d)
            ext = jnp.where(here, received[d], ext)
        return ext

    def sweep(own, ext):
        rows = [jnp.broadcast_to(ext[j : j + 1, :], (8, 128)) for j in range(8)]
        total = None
        for f in range(FACES + 1):
            product = coef_ref[8 * f] * rows[0]
            for j in range(1, 8):
                product = product + coef_ref[8 * f + j] * rows[j]
            if f == 0:
                total = COARSE_OMEGA * product
            else:
                index = jnp.broadcast_to(clane[f - 1 : f], (8, 128))
                total = total + cweight[f - 1 : f] * take(product, index)
        return own + base_c - total

    q3[...] = take(base_c, qlane)
    third = copies(2, [q3] * 4, r3)
    start_all(third)

    y_ref[...] = bf_dot(lhs_s[...], stack_right(sm_ref[...]))
    gather_faces(range(GROUPS), True)
    eye = jnp.where(
        lax.broadcasted_iota(jnp.int32, (64, 64), 0) == lax.broadcasted_iota(jnp.int32, (64, 64), 1),
        1.0,
        0.0,
    )
    left = jnp.concatenate([eye - OMEGA * comp_s[:64], comp_s[64:]], axis=0)
    products = lax.dot_general(left, prolong_t, NT, preferred_element_type=F32, precision=HIGH)
    wide_products = jnp.concatenate(
        [products[f * 64 : (f + 1) * 64] for f in range(FACES + 1)], axis=1
    )
    high, low = halves(wide_products)
    final_ref[...] = jnp.concatenate([high, low], axis=0).astype(BF16)

    for copy in third:
        copy.wait_recv()
    c1 = sweep(base_c, extend(base_c, r3))
    q4[...] = take(c1, qlane)
    fourth = copies(3, [q4] * 4, r4)
    start_all(fourth)

    gather_faces((4, 5), False)
    base_ref[...] = sm_ref[:, :512] + omega * (
        (t_ref[:64] - n_ref[...]) * inverse - y_ref[:64, :512]
    )
    code_groups = [
        jnp.broadcast_to(codes[:, s * 128 : (s + 1) * 128], (8, 128)) for s in range(GROUPS)
    ]
    for pair in range(2):
        a = ghost1[2 * pair, 32:40, :]
        b = ghost1[2 * pair + 1, 32:40, :]
        a = jnp.where(a >= 0.0, a + 512.0 * (2 * pair + 1), -1.0)
        b = jnp.where(b >= 0.0, b + 512.0 * (2 * pair + 2), -1.0)
        code_groups.append(jnp.where(lane < 64, a, b))
    for t in range(GROUPS):
        span = slice(t * 128, (t + 1) * 128)
        table = jnp.concatenate([nbr_ref[:, span], jnp.full((2, 128), -1, jnp.int32)], axis=0)
        index = table & 127
        group = table >> 7
        picked = jnp.full((8, 128), -1.0, F32)
        for s in range(GROUPS + 2):
            picked = jnp.where(group == s, take(code_groups[s], index), picked)
        codes_ref[:, span] = picked.astype(jnp.int32)
    codes_ref[6:7, :] = codes.astype(jnp.int32)

    for copy in fourth:
        copy.wait_recv()
    c2 = sweep(c1, extend(c1, r4))
    q5[...] = jnp.where(lane < 64, c2, pltpu.roll(c2, 64, 1))
    fifth = copies(4, [q5] * 4, r5)
    start_all(fifth)
    corr_ref[...] = c2[:, :64]
    for copy in fifth:
        copy.wait_recv()
    sources = (
        jnp.where(lane < 64, c2, r5[0]),
        jnp.where(lane < 64, r5[1], r5[2]),
        r5[3],
    )
    for f in range(FACES + 1):
        for t in range(GROUPS):
            span = slice(t * 128, (t + 1) * 128)
            row = codes_ref[(f + 6) % 7 : (f + 6) % 7 + 1, span]
            index = jnp.broadcast_to((row >> 3) & 127, (8, 128))
            group = jnp.broadcast_to(row >> 10, (8, 128))
            kid = jnp.broadcast_to(row & 7, (8, 128))
            kid = jnp.where(jnp.broadcast_to(row, (8, 128)) < 0, -1, kid)
            picked = jnp.zeros((8, 128), F32)
            for s in range(3 if f else 1):
                picked = jnp.where(group == s, take(sources[s], index), picked)
            if f:
                weight = face_scale_ref[f - 1 : f, span] * (omega * inverse)[:, span]
                picked = -weight * picked
            high, low = halves(picked)
            d_hi[f * 64 : (f + 1) * 64, span] = jnp.concatenate(
                [jnp.where(kid == k, high, 0.0) for k in range(8)], axis=0
            ).astype(BF16)
            d_lo[f * 64 : (f + 1) * 64, span] = jnp.concatenate(
                [jnp.where(kid == k, low, 0.0) for k in range(8)], axis=0
            ).astype(BF16)
    both = bf_dot(final_ref[...], d_hi[...])
    rest = bf_dot(final_ref[:64], d_lo[...])
    out_ref[...] = base_ref[...] + (both[:64] + both[64:] + rest)
    for group in (first, second, third, fourth, fifth):
        for copy in group:
            copy.wait_send()


def body(wide, narrow, *args):
    (
        start_field,
        right_side,
        element_scale,
        face_scale,
        face_nbr,
        send_list,
        counts,
        coarse_slot,
        elem_block,
        smooth_block,
        face_blocks,
        prolong,
        coarse_scale,
        coarse_face_scale,
        coarse_nbr,
        coarse_send,
        coarse_block,
        coarse_smooth,
        coarse_faces,
    ) = args
    vmem = pl.BlockSpec(memory_space=pltpu.VMEM)
    specs = [vmem] * len(args)
    specs[6] = pl.BlockSpec(memory_space=pltpu.SMEM)
    return tuple(
        pl.pallas_call(
            functools.partial(kernel, wide, narrow),
            out_shape=[
                jax.ShapeDtypeStruct((64, 512), F32),
                jax.ShapeDtypeStruct((8, 64), F32),
            ],
            in_specs=specs,
            out_specs=[vmem, vmem],
            scratch_shapes=[
                pltpu.VMEM((64, 512), F32),
                pltpu.VMEM((64, 768), F32),
                pltpu.VMEM((64, 512), F32),
                pltpu.VMEM((448, 768), F32),
                pltpu.VMEM((448, 192), BF16),
                pltpu.VMEM((448, 192), BF16),
                pltpu.VMEM((128, 192), BF16),
                pltpu.VMEM((448, 64), F32),
                pltpu.VMEM((448, 64), F32),
                pltpu.VMEM((128, 448), BF16),
                pltpu.VMEM((448, 512), BF16),
                pltpu.VMEM((448, 512), BF16),
                pltpu.VMEM((64, 512), F32),
                pltpu.VMEM((128, 512), F32),
                pltpu.VMEM((56, 8, 128), F32),
                pltpu.VMEM((128, 512), BF16),
                pltpu.VMEM((8, 512), jnp.int32),
                pltpu.VMEM((4, 40, 128), F32),
                pltpu.VMEM((4, 40, 128), F32),
                pltpu.VMEM((4, 32, 128), F32),
                pltpu.VMEM((4, 32, 128), F32),
                pltpu.VMEM((8, 128), F32),
                pltpu.VMEM((4, 8, 128), F32),
                pltpu.VMEM((8, 128), F32),
                pltpu.VMEM((4, 8, 128), F32),
                pltpu.VMEM((8, 128), F32),
                pltpu.VMEM((4, 8, 128), F32),
                pltpu.SemaphoreType.DMA((5, 4)),
                pltpu.SemaphoreType.DMA((5, 4)),
            ],
            compiler_params=pltpu.CompilerParams(
                collective_id=0, has_side_effects=True, vmem_limit_bytes=32 * 1024 * 1024
            ),
        )(
            start_field,
            right_side,
            element_scale.reshape(1, -1),
            face_scale,
            face_nbr,
            send_list,
            counts,
            coarse_slot.reshape(1, -1),
            elem_block,
            smooth_block,
            face_blocks,
            prolong.transpose(0, 2, 1).reshape(64, 64),
            coarse_scale.reshape(1, -1),
            coarse_face_scale,
            coarse_nbr,
            coarse_send,
            coarse_block,
            coarse_smooth,
            coarse_faces,
        )
    )


def solution(mesh):
    both = ("wide", "narrow")
    split1, split2, whole = P(both), P(None, both), P()
    return jax.shard_map(
        functools.partial(body, mesh.shape["wide"], mesh.shape["narrow"]),
        mesh=mesh,
        in_specs=(
            split2,
            split2,
            split1,
            split2,
            split2,
            split2,
            split1,
            split1,
            whole,
            whole,
            whole,
            whole,
            split1,
            split2,
            split2,
            split2,
            whole,
            whole,
            whole,
        ),
        out_specs=(split2, split2),
        check_vma=False,
    )
```

time: 166 us -> 52.8 us (0.32)
  the two profiles are of different devices: /device:TPU:1 before, /device:TPU:31 now
where the time goes in v1:
time: 52.8 us; the launch traced here: 52 us
  Pallas kernels  37.5 us (71%)
  local copies, waits for them, and re-layouts  13.2 us (25%)
  between operations  1.35 us (3%)
    pallas_call x1, Pallas kernels, body(): pl.pallas_call(functools.partial(kernel, wide, narrow), out_shape=[jax.Sh...  37.5 us
    unnamed x38, local copies, waits for them, and re-layouts  13.2 us

profile of v1, /device:TPU:31, one launch (start us, length us, event | category | flops | bytes accessed | tf_op | source)
XLA Modules:
  0.0 52.0 jit_solution(1269447793513301019)
XLA Ops:
  0.6 0.0 copy-start.10
  1.3 0.0 copy-start.9
  1.3 0.0 copy-start.17
  1.3 0.0 copy-done.10
  1.3 0.7 %copy-done.9 = f32[6,64]{1,0:T(8,128)S(1)} copy-done((f32[6,64]{1,0:T(8,128)S(1)}, f32[6,64]{1,0:T(8,128)}, u32[]{:S(2)}) %copy-start.9) | copy-done | bytes 1560
  2.0 0.0 copy-done.17
  2.0 0.0 copy-start
  2.0 0.9 %copy-done = f32[6,64,64]{2,1,0:T(8,128)S(1)} copy-done((f32[6,64,64]{2,1,0:T(8,128)S(1)}, f32[6,64,64]{2,1,0:T(8,128)}, u32[]{:S(2)}) %copy-start) | copy-done | bytes 98328
  2.9 0.0 copy-start.1
  2.9 0.9 %copy-done.1 = f32[64,512]{1,0:T(8,128)S(1)} copy-done((f32[64,512]{1,0:T(8,128)S(1)}, f32[64,512]{1,0:T(8,128)}, u32[]{:S(2)}) %copy-start.1) | copy-done | bytes 131096
  3.8 0.0 copy-start.2
  3.8 0.9 %copy-done.2 = f32[64,512]{1,0:T(8,128)S(1)} copy-done((f32[64,512]{1,0:T(8,128)S(1)}, f32[64,512]{1,0:T(8,128)}, u32[]{:S(2)}) %copy-start.2) | copy-done | bytes 131096
  4.7 0.0 copy-start.3
  4.7 0.8 %copy-done.3 = f32[64,64]{1,0:T(8,128)S(1)} copy-done((f32[64,64]{1,0:T(8,128)S(1)}, f32[64,64]{1,0:T(8,128)}, u32[]{:S(2)}) %copy-start.3) | copy-done | bytes 16408
  5.5 0.0 copy-start.4
  5.5 0.8 %copy-done.4 = f32[64,64]{1,0:T(8,128)S(1)} copy-done((f32[64,64]{1,0:T(8,128)S(1)}, f32[64,64]{1,0:T(8,128)}, u32[]{:S(2)}) %copy-start.4) | copy-done | bytes 16408
  6.3 0.0 copy-start.5
  6.3 0.8 %copy-done.5 = f32[8,64,8]{1,2,0:T(8,128)S(1)} copy-done((f32[8,64,8]{1,2,0:T(8,128)S(1)}, f32[8,64,8]{1,2,0:T(8,128)}, u32[]{:S(2)}) %copy-start.5) | copy-done | bytes 16408
  7.0 0.0 copy-start.6
  7.0 0.7 %copy-done.6 = f32[6,8,8]{2,1,0:T(8,128)S(1)} copy-done((f32[6,8,8]{2,1,0:T(8,128)S(1)}, f32[6,8,8]{2,1,0:T(8,128)}, u32[]{:S(2)}) %copy-start.6) | copy-done | bytes 1560
  7.7 0.0 copy-start.7
  7.8 0.7 %copy-done.7 = f32[6,512]{1,0:T(8,128)S(1)} copy-done((f32[6,512]{1,0:T(8,128)S(1)}, f32[6,512]{1,0:T(8,128)}, u32[]{:S(2)}) %copy-start.7) | copy-done | bytes 12312
  8.5 0.0 copy-start.8
  8.5 0.7 %copy-done.8 = s32[6,512]{1,0:T(8,128)S(1)} copy-done((s32[6,512]{1,0:T(8,128)S(1)}, s32[6,512]{1,0:T(8,128)}, u32[]{:S(2)}) %copy-start.8) | copy-done | bytes 12312
  9.2 0.0 copy-start.11
  9.2 0.7 %copy-done.11 = f32[8,8]{1,0:T(8,128)S(1)} copy-done((f32[8,8]{1,0:T(8,128)S(1)}, f32[8,8]{1,0:T(8,128)}, u32[]{:S(2)}) %copy-start.11) | copy-done | bytes 280
  9.9 0.0 copy-start.12
  9.9 0.7 %copy-done.12 = f32[8,8]{1,0:T(8,128)S(1)} copy-done((f32[8,8]{1,0:T(8,128)S(1)}, f32[8,8]{1,0:T(8,128)}, u32[]{:S(2)}) %copy-start.12) | copy-done | bytes 280
  10.6 0.0 copy-start.13
  10.6 0.7 %copy-done.13 = f32[512]{0:T(512)S(1)} copy-done((f32[512]{0:T(512)S(1)}, f32[512]{0:T(512)}, u32[]{:S(2)}) %copy-start.13) | copy-done | bytes 2072
  11.2 0.0 copy-start.14
  11.2 0.7 %copy-done.14 = s32[4,64]{1,0:T(4,128)S(1)} copy-done((s32[4,64]{1,0:T(4,128)S(1)}, s32[4,64]{1,0:T(4,128)}, u32[]{:S(2)}) %copy-start.14) | copy-done | bytes 1048
  11.9 0.0 copy-start.15
  11.9 0.7 %copy-done.15 = s32[512]{0:T(512)S(1)} copy-done((s32[512]{0:T(512)S(1)}, s32[512]{0:T(512)}, u32[]{:S(2)}) %copy-start.15) | copy-done | bytes 2072
  12.6 0.0 copy-start.16
  12.6 0.7 %copy-done.16 = s32[4,16]{1,0:T(4,128)S(1)} copy-done((s32[4,16]{1,0:T(4,128)S(1)}, s32[4,16]{1,0:T(4,128)}, u32[]{:S(2)}) %copy-start.16) | copy-done | bytes 280
  13.3 37.5 %shard_map.194 = (f32[64,512]{1,0:T(8,128)S(1)}, f32[8,64]{1,0:T(8,128)S(1)}) custom-call(f32[64,512]{1,0:T(8,128)S(1)} %copy-done.1, f32[64,512]{1,0:T(8,128)S(1)} %copy-done.2, f32[1,512]{1,0:T(1,128)S(1)} %bitcast.7, f32[6,512]{1,0:T(8,128)S(1)} %copy-done.7, s32[6,512]{1,0:T(8,128)S(1)} %copy-done.8, s32[4,64]{1,0:T(4,128)S(1)} %copy-done.14, ...), custom_call_target="tpu_custom_call" | custom-call | tf_op jit(solution)/shard_map/pallas_call | solution.py:423
  50.8 0.7 %copy.24 = f32[64,512]{1,0:T(8,128)} copy(f32[64,512]{1,0:T(8,128)S(1)} %get-tuple-element.4) | data formatting | bytes 262144
  51.4 0.6 %copy.25 = f32[8,64]{1,0:T(8,128)} copy(f32[8,64]{1,0:T(8,128)S(1)} %get-tuple-element.5) | data formatting | bytes 4096
Async XLA Ops:
  0.6 0.7 %copy-start.10 = (s32[6,64]{1,0:T(8,128)S(1)}, s32[6,64]{1,0:T(8,128)}, u32[]{:S(2)}) copy-start(s32[6,64]{1,0:T(8,128)} %cnbr_ref.1) | copy-start | bytes 4612
  1.3 0.7 %copy-start.9 = (f32[6,64]{1,0:T(8,128)S(1)}, f32[6,64]{1,0:T(8,128)}, u32[]{:S(2)}) copy-start(f32[6,64]{1,0:T(8,128)} %cface_scale_ref.1) | copy-start | bytes 4612
  1.3 0.7 %copy-start.17 = (f32[64]{0:T(128)S(1)}, f32[64]{0:T(128)}, u32[]{:S(2)}) copy-start(f32[64]{0:T(128)} %param.31) | copy-start | bytes 772
  2.0 0.9 %copy-start = (f32[6,64,64]{2,1,0:T(8,128)S(1)}, f32[6,64,64]{2,1,0:T(8,128)}, u32[]{:S(2)}) copy-start(f32[6,64,64]{2,1,0:T(8,128)} %faces_ref.1) | copy-start | bytes 294916
  2.9 0.9 %copy-start.1 = (f32[64,512]{1,0:T(8,128)S(1)}, f32[64,512]{1,0:T(8,128)}, u32[]{:S(2)}) copy-start(f32[64,512]{1,0:T(8,128)} %start_ref.1) | copy-start | bytes 393220
  3.8 0.9 %copy-start.2 = (f32[64,512]{1,0:T(8,128)S(1)}, f32[64,512]{1,0:T(8,128)}, u32[]{:S(2)}) copy-start(f32[64,512]{1,0:T(8,128)} %right_ref.1) | copy-start | bytes 393220
  4.7 0.8 %copy-start.3 = (f32[64,64]{1,0:T(8,128)S(1)}, f32[64,64]{1,0:T(8,128)}, u32[]{:S(2)}) copy-start(f32[64,64]{1,0:T(8,128)} %elem_ref.1) | copy-start | bytes 49156
  5.5 0.8 %copy-start.4 = (f32[64,64]{1,0:T(8,128)S(1)}, f32[64,64]{1,0:T(8,128)}, u32[]{:S(2)}) copy-start(f32[64,64]{1,0:T(8,128)} %smooth_ref.1) | copy-start | bytes 49156
  6.3 0.8 %copy-start.5 = (f32[8,64,8]{1,2,0:T(8,128)S(1)}, f32[8,64,8]{1,2,0:T(8,128)}, u32[]{:S(2)}) copy-start(f32[8,64,8]{1,2,0:T(8,128)} %param.30) | copy-start | bytes 49156
  7.0 0.7 %copy-start.6 = (f32[6,8,8]{2,1,0:T(8,128)S(1)}, f32[6,8,8]{2,1,0:T(8,128)}, u32[]{:S(2)}) copy-start(f32[6,8,8]{2,1,0:T(8,128)} %cfaces_ref.1) | copy-start | bytes 4612
  7.7 0.7 %copy-start.7 = (f32[6,512]{1,0:T(8,128)S(1)}, f32[6,512]{1,0:T(8,128)}, u32[]{:S(2)}) copy-start(f32[6,512]{1,0:T(8,128)} %face_scale_ref.1) | copy-start | bytes 36868
  8.5 0.7 %copy-start.8 = (s32[6,512]{1,0:T(8,128)S(1)}, s32[6,512]{1,0:T(8,128)}, u32[]{:S(2)}) copy-start(s32[6,512]{1,0:T(8,128)} %nbr_ref.1) | copy-start | bytes 36868
  9.2 0.7 %copy-start.11 = (f32[8,8]{1,0:T(8,128)S(1)}, f32[8,8]{1,0:T(8,128)}, u32[]{:S(2)}) copy-start(f32[8,8]{1,0:T(8,128)} %cblock_ref.1) | copy-start | bytes 772
  9.9 0.7 %copy-start.12 = (f32[8,8]{1,0:T(8,128)S(1)}, f32[8,8]{1,0:T(8,128)}, u32[]{:S(2)}) copy-start(f32[8,8]{1,0:T(8,128)} %csmooth_ref.1) | copy-start | bytes 772
  10.6 0.7 %copy-start.13 = (f32[512]{0:T(512)S(1)}, f32[512]{0:T(512)}, u32[]{:S(2)}) copy-start(f32[512]{0:T(512)} %param.21) | copy-start | bytes 6148
  11.2 0.7 %copy-start.14 = (s32[4,64]{1,0:T(4,128)S(1)}, s32[4,64]{1,0:T(4,128)}, u32[]{:S(2)}) copy-start(s32[4,64]{1,0:T(4,128)} %send_ref.1) | copy-start | bytes 3076
  11.9 0.7 %copy-start.15 = (s32[512]{0:T(512)S(1)}, s32[512]{0:T(512)}, u32[]{:S(2)}) copy-start(s32[512]{0:T(512)} %param.26) | copy-start | bytes 6148
  12.6 0.7 %copy-start.16 = (s32[4,16]{1,0:T(4,128)S(1)}, s32[4,16]{1,0:T(4,128)}, u32[]{:S(2)}) copy-start(s32[4,16]{1,0:T(4,128)} %csend_ref.1) | copy-start | bytes 772

commit v2 on v1

--- a/solution.py
+++ b/solution.py
@@ -15,6 +15,14 @@
 FACES = 6
 GROUPS = 4
 NT = (((1,), (1,)), ((), ()))
+SOURCES = ((-1, 0), (1, 0), (0, -1), (0, 1))
+RANGE = range(-3, 4)
+BALL = sorted(
+    ((a, b) for a in RANGE for b in RANGE if 0 < abs(a) + abs(b) <= 3),
+    key=lambda o: (-abs(o[0]) - abs(o[1]), o),
+)
+NEAR = ((0, 0),) + SOURCES
+NEXT = NEAR + ((-2, 0), (-1, -1), (-1, 1), (2, 0), (1, -1), (1, 1), (0, -2), (0, 2))
 
 
 def take(values, lanes):
@@ -48,25 +56,25 @@
 def kernel(
     wide,
     narrow,
-    start_ref,
-    right_ref,
-    scale_ref,
-    face_scale_ref,
-    nbr_ref,
-    send_ref,
-    counts_ref,
-    slot_ref,
-    elem_ref,
-    smooth_ref,
-    faces_ref,
-    prolong_ref,
-    cscale_ref,
-    cface_scale_ref,
-    cnbr_ref,
-    csend_ref,
-    cblock_ref,
-    csmooth_ref,
-    cfaces_ref,
+    start_hbm,
+    right_hbm,
+    scale_hbm,
+    face_scale_hbm,
+    nbr_hbm,
+    send_hbm,
+    counts_hbm,
+    slot_hbm,
+    elem_hbm,
+    smooth_hbm,
+    faces_hbm,
+    prolong_hbm,
+    cscale_hbm,
+    cface_scale_hbm,
+    cnbr_hbm,
+    csend_hbm,
+    cblock_hbm,
+    csmooth_hbm,
+    cfaces_hbm,
     out_ref,
     corr_ref,
     x_ref,
@@ -90,15 +98,71 @@
     ghost1,
     pack2,
     ghost2,
-    q3,
-    r3,
-    q4,
-    r4,
-    q5,
-    r5,
+    pack2n,
+    ghost2n,
+    tile3,
+    ghost3,
+    clane_ref,
+    cweight_ref,
+    qlane_ref,
     send_sem,
     recv_sem,
+    send_sem3,
+    recv_sem3,
+    start_ref,
+    right_ref,
+    scale_ref,
+    face_scale_ref,
+    nbr_ref,
+    send_ref,
+    slot_ref,
+    elem_ref,
+    smooth_ref,
+    faces_ref,
+    prolong_ref,
+    cscale_ref,
+    cface_scale_ref,
+    cnbr_ref,
+    csend_ref,
+    cblock_ref,
+    csmooth_ref,
+    cfaces_ref,
+    counts_ref,
+    load_sem,
 ):
+    loads = {
+        name: pltpu.make_async_copy(source, target, load_sem.at[i])
+        for i, (name, source, target) in enumerate(
+            (
+                ("send", send_hbm, send_ref),
+                ("counts", counts_hbm, counts_ref),
+                ("start", start_hbm, start_ref),
+                ("slot", slot_hbm, slot_ref),
+                ("right", right_hbm, right_ref),
+                ("scale", scale_hbm, scale_ref),
+                ("face_scale", face_scale_hbm, face_scale_ref),
+                ("nbr", nbr_hbm, nbr_ref),
+                ("elem", elem_hbm, elem_ref),
+                ("smooth", smooth_hbm, smooth_ref),
+                ("faces", faces_hbm, faces_ref),
+                ("prolong", prolong_hbm, prolong_ref),
+                ("cscale", cscale_hbm, cscale_ref),
+                ("cface_scale", cface_scale_hbm, cface_scale_ref),
+                ("cnbr", cnbr_hbm, cnbr_ref),
+                ("csend", csend_hbm, csend_ref),
+                ("cblock", cblock_hbm, cblock_ref),
+                ("csmooth", csmooth_hbm, csmooth_ref),
+                ("cfaces", cfaces_hbm, cfaces_ref),
+            )
+        )
+    }
+    for load in loads.values():
+        load.start()
+
+    def arrive(*names):
+        for name in names:
+            loads[name].wait()
+
     me_w = lax.axis_index("wide")
     me_n = lax.axis_index("narrow")
     targets = (
@@ -117,13 +181,11 @@
     lane1 = lax.broadcasted_iota(jnp.int32, (1, 128), 1)
     low32 = jnp.broadcast_to(lane1 < 64, (32, 128))
     element = lax.broadcasted_iota(jnp.int32, (1, 512), 1)
-    active = jnp.where(element < counts_ref[0], 1.0, 0.0).astype(F32)
-
     def copies(step, sources, buffers):
         return [
             pltpu.make_async_remote_copy(
                 src_ref=sources[d],
-                dst_ref=buffers.at[d],
+                dst_ref=buffers[d],
                 send_sem=send_sem.at[step, d],
                 recv_sem=recv_sem.at[step, d],
                 device_id=targets[d],
@@ -136,12 +198,14 @@
         for d in (2, 3, 0, 1):
             group[d].start()
 
-    def pack(field_ref, packets, codes=None):
+    def send_row(pair):
+        return jnp.concatenate(
+            [send_ref[2 * pair : 2 * pair + 1, :], send_ref[2 * pair + 1 : 2 * pair + 2, :]], axis=1
+        )
+
+    def pack(field_ref, packets):
         for pair in range(2):
-            row = jnp.concatenate(
-                [send_ref[2 * pair : 2 * pair + 1, :], send_ref[2 * pair + 1 : 2 * pair + 2, :]],
-                axis=1,
-            )
+            row = send_row(pair)
             index = jnp.broadcast_to(row & 127, (64, 128))
             group = jnp.broadcast_to(row >> 7, (64, 128))
             picked = jnp.zeros((64, 128), F32)
@@ -149,24 +213,14 @@
                 got = take(field_ref[:, s * 128 : (s + 1) * 128], index)
                 picked = jnp.where(group == s, got, picked)
             moved = pltpu.roll(picked[32:], 64, 1)
-            packets[2 * pair, 0:32, :] = jnp.where(low32, picked[:32], moved)
-            packets[2 * pair + 1, 0:32, :] = jnp.where(low32, moved, picked[:32])
-            if codes is not None:
-                picked = jnp.zeros((8, 128), F32)
-                for s in range(GROUPS):
-                    got = take(
-                        jnp.broadcast_to(codes[:, s * 128 : (s + 1) * 128], (8, 128)),
-                        index[:8],
-                    )
-                    picked = jnp.where(group[:8] == s, got, picked)
-                packets[2 * pair, 32:40, :] = picked
-                packets[2 * pair + 1, 32:40, :] = picked
+            packets[2 * pair][0:32, :] = jnp.where(low32, picked[:32], moved)
+            packets[2 * pair + 1][0:32, :] = jnp.where(low32, moved, picked[:32])
 
     def unpack(ghosts):
         columns = []
         for pair in range(2):
-            a = ghosts[2 * pair, 0:32, :]
-            b = ghosts[2 * pair + 1, 0:32, :]
+            a = ghosts[2 * pair][0:32, :]
+            b = ghosts[2 * pair + 1][0:32, :]
             first = jnp.where(low32, a, b)
             second = pltpu.roll(jnp.where(low32, b, a), 64, 1)
             columns.append(jnp.concatenate([first, second], axis=0))
@@ -189,13 +243,39 @@
                 total = total + face_scale_ref[f : f + 1, span] * picked
             n_ref[:, span] = total
 
+    arrive("counts", "send", "start", "slot", "cscale", "cface_scale", "cnbr", "csend")
+    active = jnp.where(element < counts_ref[0, 0], 1.0, 0.0).astype(F32)
     x_ref[...] = start_ref[...] * active
     codes = jnp.where(active > 0.0, slot_ref[...].astype(F32), -1.0)
-    pack(x_ref, pack1, codes)
+    cinv = COARSE_OMEGA / jnp.concatenate([cscale_ref[...]] * 2, axis=1)
+    cnbr = cnbr_ref[...]
+    weights = jnp.where(cnbr >= 0, cface_scale_ref[...], 0.0) * cinv[:, :64]
+    csend = csend_ref[...]
+    static = jnp.concatenate(
+        [
+            jnp.concatenate([jnp.maximum(cnbr, 0).astype(F32), weights], axis=1),
+            jnp.concatenate([csend[d : d + 1] for d in range(4)] * 2, axis=1).astype(F32),
+        ],
+        axis=0,
+    )
+    pack(x_ref, [pack1.at[d] for d in range(4)])
+    for pair in range(2):
+        row = send_row(pair)
+        index = jnp.broadcast_to(row & 127, (8, 128))
+        group = jnp.broadcast_to(row >> 7, (8, 128))
+        picked = jnp.zeros((8, 128), F32)
+        for s in range(GROUPS):
+            span = slice(s * 128, (s + 1) * 128)
+            got = take(jnp.broadcast_to(codes[:, span], (8, 128)), index)
+            picked = jnp.where(group == s, got, picked)
+        tile = jnp.concatenate([static, picked[:1]], axis=0)
+        pack1[2 * pair, 32:40, :] = tile
+        pack1[2 * pair + 1, 32:40, :] = tile
     pl.semaphore_wait(barrier, 4)
-    first = copies(0, [pack1.at[d] for d in range(4)], ghost1)
+    first = copies(0, [pack1.at[d] for d in range(4)], [ghost1.at[d] for d in range(4)])
     start_all(first)
 
+    arrive("smooth", "elem", "faces", "nbr", "face_scale", "csmooth", "prolong", "right", "scale")
     smooth = smooth_ref[...]
     csmooth = csmooth_ref[...]
     prolong_t = prolong_ref[...]
@@ -218,11 +298,16 @@
 
     for copy in first:
         copy.wait_recv()
-    y_ref[64:, 512:] = bf_dot(lhs_s[64:, :], stack_right(unpack(ghost1)))
+    y_ref[64:, 512:] = bf_dot(lhs_s[64:, :], stack_right(unpack([ghost1.at[d] for d in range(4)])))
     gather_faces((4, 5), False)
     sm_ref[:, :512] = x_ref[...] + omega * ((t_ref[:64] - n_ref[...]) * inverse - y_ref[:64, :512])
-    pack(sm_ref, pack2)
-    second = copies(1, [pack2.at[d] for d in range(4)], ghost2)
+    packets2 = [pack2.at[0], pack2.at[1], pack2n.at[0], pack2n.at[1]]
+    arrived2 = [ghost2.at[0], ghost2.at[1], ghost2n.at[0], ghost2n.at[1]]
+    pack(sm_ref, packets2)
+    for d in range(4):
+        for i, source in enumerate((d, 2, 3) if d < 2 else (d,)):
+            packets2[d][32 + 8 * i : 40 + 8 * i, :] = ghost1[source, 32:40, :]
+    second = copies(1, packets2, arrived2)
     start_all(second)
 
     for f in range(FACES + 1):
@@ -232,6 +317,7 @@
     y_ref[:, :512] = bf_dot(lhs_p[...], stack_right(sm_ref[:, :512]))
     gather_faces(range(GROUPS), True)
     n_ref[...] = active * t_ref[64:] - scale_ref[...] * y_ref[:64, :512] - n_ref[...]
+    arrive("cblock", "cfaces")
     together = jnp.concatenate([cblock_ref[...]] + [cfaces_ref[f] for f in range(FACES)], axis=1)
     coarse = exact_dot(csmooth, together)
     for c in range(8 * (FACES + 1)):
@@ -240,18 +326,19 @@
     child = slot_ref[...] & 7
     row128 = lax.broadcasted_iota(jnp.int32, (128, 512), 0) & 63
     onehot_ref[...] = jnp.where(row128 == parent, 1.0, 0.0).astype(BF16)
-    cinv = COARSE_OMEGA / jnp.concatenate([cscale_ref[...]] * 2, axis=1)
-    cnbr = jnp.concatenate([cnbr_ref[...]] * 2, axis=1)
-    cweight = jnp.concatenate([cface_scale_ref[...]] * 2, axis=1)
-    cweight = jnp.where(cnbr >= 0, cweight, 0.0) * cinv
-    clane = jnp.maximum(cnbr, 0)
-    csend = csend_ref[...]
-    row = jnp.concatenate([csend[d : d + 1] for d in range(4)] * 2, axis=1)
-    qlane = jnp.broadcast_to(row, (8, 128))
+
+    def keep_static(i, tile):
+        clane_ref[i] = tile.astype(jnp.int32)
+        cweight_ref[i] = pltpu.roll(tile, 64, 1)
+        qlane_ref[i] = jnp.broadcast_to(tile[6:7], (8, 128)).astype(jnp.int32)
+
+    keep_static(0, pack1[0, 32:40, :])
+    for d in range(4):
+        keep_static(1 + d, ghost1[d, 32:40, :])
 
     for copy in second:
         copy.wait_recv()
-    sm_ref[:, 512:] = unpack(ghost2)
+    sm_ref[:, 512:] = unpack(arrived2)
     y_ref[64:, 512:] = bf_dot(lhs_p[64:, :], stack_right(sm_ref[:, 512:]))
 
     def minus_faces():
@@ -280,14 +367,14 @@
     summed = lax.dot_general(both, onehot_ref[...], NT, preferred_element_type=F32)
     base_c = (summed[:8] + summed[8:]) * cinv
 
-    def extend(own, received):
-        ext = own
-        for d in range(4):
+    def extend(parts, at):
+        ext = parts[at]
+        for d, (a, b) in enumerate(SOURCES):
             here = (lane >= 64 + 16 * d) & (lane < 80 + 16 * d)
-            ext = jnp.where(here, received[d], ext)
+            ext = jnp.where(here, parts[(at[0] + a, at[1] + b)], ext)
         return ext
 
-    def sweep(own, ext):
+    def sweep(own, right, ext, i):
         rows = [jnp.broadcast_to(ext[j : j + 1, :], (8, 128)) for j in range(8)]
         total = None
         for f in range(FACES + 1):
@@ -297,13 +384,27 @@
             if f == 0:
                 total = COARSE_OMEGA * product
             else:
-                index = jnp.broadcast_to(clane[f - 1 : f], (8, 128))
-                total = total + cweight[f - 1 : f] * take(product, index)
-        return own + base_c - total
-
-    q3[...] = take(base_c, qlane)
-    third = copies(2, [q3] * 4, r3)
-    start_all(third)
+                index = jnp.broadcast_to(clane_ref[i, f - 1 : f, :], (8, 128))
+                total = total + cweight_ref[i, f - 1 : f, :] * take(product, index)
+        return own + right - total
+
+    tile3[...] = jnp.where(lane < 64, base_c, take(base_c, qlane_ref[0]))
+    third = [
+        pltpu.make_async_remote_copy(
+            src_ref=tile3,
+            dst_ref=ghost3.at[BALL.index((-a, -b))],
+            send_sem=send_sem3.at[i],
+            recv_sem=recv_sem3.at[BALL.index((-a, -b))],
+            device_id={
+                "wide": lax.rem(me_w + (a + wide), wide),
+                "narrow": lax.rem(me_n + (b + narrow), narrow),
+            },
+            device_id_type=pl.DeviceIdType.MESH,
+        )
+        for i, (a, b) in enumerate(BALL)
+    ]
+    for copy in third:
+        copy.start()
 
     y_ref[...] = bf_dot(lhs_s[...], stack_right(sm_ref[...]))
     gather_faces(range(GROUPS), True)
@@ -320,13 +421,10 @@
     high, low = halves(wide_products)
     final_ref[...] = jnp.concatenate([high, low], axis=0).astype(BF16)
 
-    for copy in third:
-        copy.wait_recv()
-    c1 = sweep(base_c, extend(base_c, r3))
-    q4[...] = take(c1, qlane)
-    fourth = copies(3, [q4] * 4, r4)
-    start_all(fourth)
-
+    for d in range(2):
+        for i in range(3):
+            keep_static(5 + 3 * d + i, ghost2[d, 32 + 8 * i : 40 + 8 * i, :])
+        keep_static(11 + d, ghost2n[d, 32:40, :])
     gather_faces((4, 5), False)
     base_ref[...] = sm_ref[:, :512] + omega * (
         (t_ref[:64] - n_ref[...]) * inverse - y_ref[:64, :512]
@@ -335,8 +433,8 @@
         jnp.broadcast_to(codes[:, s * 128 : (s + 1) * 128], (8, 128)) for s in range(GROUPS)
     ]
     for pair in range(2):
-        a = ghost1[2 * pair, 32:40, :]
-        b = ghost1[2 * pair + 1, 32:40, :]
+        a = jnp.broadcast_to(ghost1[2 * pair, 39:40, :], (8, 128))
+        b = jnp.broadcast_to(ghost1[2 * pair + 1, 39:40, :], (8, 128))
         a = jnp.where(a >= 0.0, a + 512.0 * (2 * pair + 1), -1.0)
         b = jnp.where(b >= 0.0, b + 512.0 * (2 * pair + 2), -1.0)
         code_groups.append(jnp.where(lane < 64, a, b))
@@ -351,19 +449,21 @@
         codes_ref[:, span] = picked.astype(jnp.int32)
     codes_ref[6:7, :] = codes.astype(jnp.int32)
 
-    for copy in fourth:
+    for copy in third:
         copy.wait_recv()
-    c2 = sweep(c1, extend(c1, r4))
-    q5[...] = jnp.where(lane < 64, c2, pltpu.roll(c2, 64, 1))
-    fifth = copies(4, [q5] * 4, r5)
-    start_all(fifth)
-    corr_ref[...] = c2[:, :64]
-    for copy in fifth:
-        copy.wait_recv()
+    parts0 = {(0, 0): tile3[...]}
+    for i, offset in enumerate(BALL):
+        parts0[offset] = ghost3[i]
+    once, parts1 = {}, {}
+    for i, at in enumerate(NEXT):
+        once[at] = sweep(parts0[at], parts0[at], extend(parts0, at), i)
+        parts1[at] = jnp.where(lane < 64, once[at], take(once[at], qlane_ref[i]))
+    c2 = [sweep(once[at], parts0[at], extend(parts1, at), i) for i, at in enumerate(NEAR)]
+    corr_ref[...] = c2[0][:, :64]
     sources = (
-        jnp.where(lane < 64, c2, r5[0]),
-        jnp.where(lane < 64, r5[1], r5[2]),
-        r5[3],
+        jnp.where(lane < 64, c2[0], pltpu.roll(c2[1], 64, 1)),
+        jnp.where(lane < 64, c2[2], pltpu.roll(c2[3], 64, 1)),
+        c2[4],
     )
     for f in range(FACES + 1):
         for t in range(GROUPS):
@@ -389,7 +489,7 @@
     both = bf_dot(final_ref[...], d_hi[...])
     rest = bf_dot(final_ref[:64], d_lo[...])
     out_ref[...] = base_ref[...] + (both[:64] + both[64:] + rest)
-    for group in (first, second, third, fourth, fifth):
+    for group in (first, second, third):
         for copy in group:
             copy.wait_send()
 
@@ -417,14 +517,13 @@
         coarse_faces,
     ) = args
     vmem = pl.BlockSpec(memory_space=pltpu.VMEM)
-    specs = [vmem] * len(args)
-    specs[6] = pl.BlockSpec(memory_space=pltpu.SMEM)
+    specs = [pl.BlockSpec(memory_space=pltpu.HBM)] * len(args)
     return tuple(
         pl.pallas_call(
             functools.partial(kernel, wide, narrow),
             out_shape=[
-                jax.ShapeDtypeStruct((64, 512), F32),
-                jax.ShapeDtypeStruct((8, 64), F32),
+                pltpu.VMEM((64, 512), F32),
+                pltpu.VMEM((8, 64), F32),
             ],
             in_specs=specs,
             out_specs=[vmem, vmem],
@@ -448,19 +547,42 @@
                 pltpu.VMEM((8, 512), jnp.int32),
                 pltpu.VMEM((4, 40, 128), F32),
                 pltpu.VMEM((4, 40, 128), F32),
-                pltpu.VMEM((4, 32, 128), F32),
-                pltpu.VMEM((4, 32, 128), F32),
+                pltpu.VMEM((2, 56, 128), F32),
+                pltpu.VMEM((2, 56, 128), F32),
+                pltpu.VMEM((2, 40, 128), F32),
+                pltpu.VMEM((2, 40, 128), F32),
                 pltpu.VMEM((8, 128), F32),
-                pltpu.VMEM((4, 8, 128), F32),
-                pltpu.VMEM((8, 128), F32),
-                pltpu.VMEM((4, 8, 128), F32),
-                pltpu.VMEM((8, 128), F32),
-                pltpu.VMEM((4, 8, 128), F32),
-                pltpu.SemaphoreType.DMA((5, 4)),
-                pltpu.SemaphoreType.DMA((5, 4)),
+                pltpu.VMEM((24, 8, 128), F32),
+                pltpu.VMEM((13, 8, 128), jnp.int32),
+                pltpu.VMEM((13, 8, 128), F32),
+                pltpu.VMEM((13, 8, 128), jnp.int32),
+                pltpu.SemaphoreType.DMA((2, 4)),
+                pltpu.SemaphoreType.DMA((2, 4)),
+                pltpu.SemaphoreType.DMA((24,)),
+                pltpu.SemaphoreType.DMA((24,)),
+                pltpu.VMEM((64, 512), F32),
+                pltpu.VMEM((64, 512), F32),
+                pltpu.VMEM((1, 512), F32),
+                pltpu.VMEM((6, 512), F32),
+                pltpu.VMEM((6, 512), jnp.int32),
+                pltpu.VMEM((4, 64), jnp.int32),
+                pltpu.VMEM((1, 512), jnp.int32),
+                pltpu.VMEM((64, 64), F32),
+                pltpu.VMEM((64, 64), F32),
+                pltpu.VMEM((6, 64, 64), F32),
+                pltpu.VMEM((64, 64), F32),
+                pltpu.VMEM((1, 64), F32),
+                pltpu.VMEM((6, 64), F32),
+                pltpu.VMEM((6, 64), jnp.int32),
+                pltpu.VMEM((4, 16), jnp.int32),
+                pltpu.VMEM((8, 8), F32),
+                pltpu.VMEM((8, 8), F32),
+                pltpu.VMEM((6, 8, 8), F32),
+                pltpu.SMEM((1, 1), jnp.int32),
+                pltpu.SemaphoreType.DMA((19,)),
             ],
             compiler_params=pltpu.CompilerParams(
-                collective_id=0, has_side_effects=True, vmem_limit_bytes=32 * 1024 * 1024
+                collective_id=0, has_side_effects=True, vmem_limit_bytes=60 * 1024 * 1024
             ),
         )(
             start_field,
@@ -469,7 +591,7 @@
             face_scale,
             face_nbr,
             send_list,
-            counts,
+            counts.reshape(1, 1),
             coarse_slot.reshape(1, -1),
             elem_block,
             smooth_block,

time: 52.8 us -> 37 us (0.70)
  the two profiles are of different devices: /device:TPU:31 before, /device:TPU:1 now
where the time goes in v2:
time: 37 us; the launch traced here: 36.9 us
  Pallas kernels  34.3 us (93%)
  between operations  1.29 us (3%)
  local copies, waits for them, and re-layouts  1.25 us (3%)
    pallas_call x1, Pallas kernels, body(): pl.pallas_call(functools.partial(kernel, wide, narrow), out_shape=[pltpu....  34.3 us
    unnamed x2, local copies, waits for them, and re-layouts  1.25 us

profile of v2, /device:TPU:1, one launch (start us, length us, event | category | flops | bytes accessed | tf_op | source)
XLA Modules:
  0.0 36.9 jit_solution(5242182941691001872)
XLA Ops:
  1.3 34.3 %shard_map.194 = (f32[64,512]{1,0:T(8,128)S(1)}, f32[8,64]{1,0:T(8,128)S(1)}) custom-call(f32[64,512]{1,0:T(8,128)} %start_hbm.1, f32[64,512]{1,0:T(8,128)} %right_hbm.1, f32[1,512]{1,0:T(1,128)} %bitcast.9, f32[6,512]{1,0:T(8,128)} %face_scale_hbm.1, s32[6,512]{1,0:T(8,128)} %nbr_hbm.1, s32[4,64]{1,0:T(4,128)} %send_hbm.1, s32[1,1]{1,0:T(1,128)} %bitcast.7.counts_hbm, ...), custom_call_target="tpu_custom_call" | custom-call | tf_op jit(solution)/shard_map/pallas_call | solution.py:522
  35.6 0.7 %copy.23 = f32[64,512]{1,0:T(8,128)} copy(f32[64,512]{1,0:T(8,128)S(1)} %get-tuple-element.2) | data formatting | bytes 262144
  36.3 0.6 %copy.24 = f32[8,64]{1,0:T(8,128)} copy(f32[8,64]{1,0:T(8,128)S(1)} %get-tuple-element.3) | data formatting | bytes 4096

commit v3 on v2

--- a/solution.py
+++ b/solution.py
@@ -92,7 +92,11 @@
     base_ref,
     t_ref,
     coef_ref,
-    onehot_ref,
+    sent_ref,
+    sent_ghost,
+    sent_weight,
+    child_ghost,
+    child_weight,
     codes_ref,
     pack1,
     ghost1,
@@ -181,6 +185,7 @@
     lane1 = lax.broadcasted_iota(jnp.int32, (1, 128), 1)
     low32 = jnp.broadcast_to(lane1 < 64, (32, 128))
     element = lax.broadcasted_iota(jnp.int32, (1, 512), 1)
+
     def copies(step, sources, buffers):
         return [
             pltpu.make_async_remote_copy(
@@ -203,18 +208,28 @@
             [send_ref[2 * pair : 2 * pair + 1, :], send_ref[2 * pair + 1 : 2 * pair + 2, :]], axis=1
         )
 
-    def pack(field_ref, packets):
-        for pair in range(2):
-            row = send_row(pair)
-            index = jnp.broadcast_to(row & 127, (64, 128))
-            group = jnp.broadcast_to(row >> 7, (64, 128))
-            picked = jnp.zeros((64, 128), F32)
-            for s in range(GROUPS):
-                got = take(field_ref[:, s * 128 : (s + 1) * 128], index)
-                picked = jnp.where(group == s, got, picked)
-            moved = pltpu.roll(picked[32:], 64, 1)
-            packets[2 * pair][0:32, :] = jnp.where(low32, picked[:32], moved)
-            packets[2 * pair + 1][0:32, :] = jnp.where(low32, moved, picked[:32])
+    def at_sends(pair, groups):
+        rows = groups[0].shape[0]
+        row = send_row(pair)
+        index = jnp.broadcast_to(row & 127, (rows, 128))
+        group = jnp.broadcast_to(row >> 7, (rows, 128))
+        picked = jnp.zeros((rows, 128), F32)
+        for s in range(GROUPS):
+            picked = jnp.where(group == s, take(groups[s], index), picked)
+        return picked
+
+    def lane_groups(x):
+        return [x[:, s * 128 : (s + 1) * 128] for s in range(GROUPS)]
+
+    def fill(pair, picked, packets):
+        moved = pltpu.roll(picked[32:], 64, 1)
+        packets[2 * pair][0:32, :] = jnp.where(low32, picked[:32], moved)
+        packets[2 * pair + 1][0:32, :] = jnp.where(low32, moved, picked[:32])
+
+    def from_ghosts(rows, row):
+        index = jnp.broadcast_to(row & 127, (rows.stop - rows.start, 128))
+        second = jnp.broadcast_to(row >= 128, (rows.stop - rows.start, 128))
+        return jnp.where(second, take(y_ref[rows, 640:768], index), take(y_ref[rows, 512:640], index))
 
     def unpack(ghosts):
         columns = []
@@ -258,16 +273,9 @@
         ],
         axis=0,
     )
-    pack(x_ref, [pack1.at[d] for d in range(4)])
     for pair in range(2):
-        row = send_row(pair)
-        index = jnp.broadcast_to(row & 127, (8, 128))
-        group = jnp.broadcast_to(row >> 7, (8, 128))
-        picked = jnp.zeros((8, 128), F32)
-        for s in range(GROUPS):
-            span = slice(s * 128, (s + 1) * 128)
-            got = take(jnp.broadcast_to(codes[:, span], (8, 128)), index)
-            picked = jnp.where(group == s, got, picked)
+        fill(pair, at_sends(pair, lane_groups(x_ref)), [pack1.at[d] for d in range(4)])
+        picked = at_sends(pair, [jnp.broadcast_to(c, (8, 128)) for c in lane_groups(codes)])
         tile = jnp.concatenate([static, picked[:1]], axis=0)
         pack1[2 * pair, 32:40, :] = tile
         pack1[2 * pair + 1, 32:40, :] = tile
@@ -296,20 +304,50 @@
     inverse = 1.0 / scale_ref[...]
     omega = OMEGA * active
 
+    step = -omega * inverse
+    sm_ref[:, :512] = x_ref[...] + omega * (t_ref[:64] * inverse - y_ref[:64, :512]) + step * n_ref[...]
+    nbr = nbr_ref[...]
+    remote = nbr >= 512
+    ghost = jnp.where(remote, nbr - 512, 0).astype(F32)
+    weight = jnp.where(remote, face_scale_ref[...], 0.0)
+    blank = jnp.zeros((2, 512), F32)
+    ghost = jnp.concatenate([ghost, blank], axis=0)
+    weight = jnp.concatenate([weight, blank], axis=0)
+    for pair in range(2):
+        span = slice(pair * 128, (pair + 1) * 128)
+        sent_ref[:, span] = at_sends(pair, lane_groups(sm_ref))
+        sent_ghost[:, span] = at_sends(pair, lane_groups(ghost)).astype(jnp.int32)
+        sent_weight[:, span] = at_sends(pair, lane_groups(step * weight))
+    slot = slot_ref[...]
+    place = (slot & 7) * 64 + (slot >> 3)
+    order = jnp.where(lax.broadcasted_iota(jnp.int32, (512, 512), 0) == place, 1.0, 0.0).astype(BF16)
+    high, rest = halves(weight)
+    middle, low = halves(rest)
+    tables = jnp.concatenate([ghost, high, middle, low], axis=0).astype(BF16)
+    ordered = lax.dot_general(tables, order, NT, preferred_element_type=F32)
+    child_ghost[...] = ordered[:8].astype(jnp.int32)
+    child_weight[...] = ordered[8:16] + (ordered[16:24] + ordered[24:])
+
     for copy in first:
         copy.wait_recv()
     y_ref[64:, 512:] = bf_dot(lhs_s[64:, :], stack_right(unpack([ghost1.at[d] for d in range(4)])))
-    gather_faces((4, 5), False)
-    sm_ref[:, :512] = x_ref[...] + omega * ((t_ref[:64] - n_ref[...]) * inverse - y_ref[:64, :512])
     packets2 = [pack2.at[0], pack2.at[1], pack2n.at[0], pack2n.at[1]]
     arrived2 = [ghost2.at[0], ghost2.at[1], ghost2n.at[0], ghost2n.at[1]]
-    pack(sm_ref, packets2)
     for d in range(4):
         for i, source in enumerate((d, 2, 3) if d < 2 else (d,)):
             packets2[d][32 + 8 * i : 40 + 8 * i, :] = ghost1[source, 32:40, :]
+    for pair in range(2):
+        span = slice(pair * 128, (pair + 1) * 128)
+        total = sent_ref[:, span]
+        for f in range(FACES):
+            found = from_ghosts(slice((f + 1) * 64, (f + 2) * 64), sent_ghost[f : f + 1, span])
+            total = total + sent_weight[f : f + 1, span] * found
+        fill(pair, total, packets2)
     second = copies(1, packets2, arrived2)
     start_all(second)
 
+    gather_faces((4, 5), True)
+    sm_ref[:, :512] = sm_ref[:, :512] + step * n_ref[...]
     for f in range(FACES + 1):
         block = elem_ref[...] if f == 0 else faces_ref[f - 1]
         comp_p[f * 64 : (f + 1) * 64, :] = exact_dot(restrict, block)
@@ -317,15 +355,21 @@
     y_ref[:, :512] = bf_dot(lhs_p[...], stack_right(sm_ref[:, :512]))
     gather_faces(range(GROUPS), True)
     n_ref[...] = active * t_ref[64:] - scale_ref[...] * y_ref[:64, :512] - n_ref[...]
+    child = slot & 7
+    chosen = jnp.zeros((8, 512), F32)
+    for k in range(8):
+        chosen = jnp.where(child == k, n_ref[8 * k : 8 * k + 8, :], chosen)
+    row128 = lax.broadcasted_iota(jnp.int32, (128, 512), 0) & 63
+    onehot = jnp.where(row128 == (slot >> 3), 1.0, 0.0).astype(BF16)
+    high, low = halves(chosen)
+    both = jnp.concatenate([high, low], axis=0).astype(BF16)
+    summed = lax.dot_general(both, onehot, NT, preferred_element_type=F32)
+    local_c = summed[:8] + summed[8:]
     arrive("cblock", "cfaces")
     together = jnp.concatenate([cblock_ref[...]] + [cfaces_ref[f] for f in range(FACES)], axis=1)
     coarse = exact_dot(csmooth, together)
     for c in range(8 * (FACES + 1)):
         coef_ref[c] = jnp.broadcast_to(coarse[:, c : c + 1], (8, 128))
-    parent = slot_ref[...] >> 3
-    child = slot_ref[...] & 7
-    row128 = lax.broadcasted_iota(jnp.int32, (128, 512), 0) & 63
-    onehot_ref[...] = jnp.where(row128 == parent, 1.0, 0.0).astype(BF16)
 
     def keep_static(i, tile):
         clane_ref[i] = tile.astype(jnp.int32)
@@ -341,31 +385,16 @@
     sm_ref[:, 512:] = unpack(arrived2)
     y_ref[64:, 512:] = bf_dot(lhs_p[64:, :], stack_right(sm_ref[:, 512:]))
 
-    def minus_faces():
-        for t in range(GROUPS):
-            span = slice(t * 128, (t + 1) * 128)
-            total = n_ref[:, span]
-            for f in range(FACES):
-                row = nbr_ref[f : f + 1, span]
-                index = jnp.broadcast_to(row & 127, (64, 128))
-                group = jnp.broadcast_to(row >> 7, (64, 128))
-                picked = jnp.zeros((64, 128), F32)
-                for s in (4, 5):
-                    got = take(
-                        y_ref[(f + 1) * 64 : (f + 2) * 64, s * 128 : (s + 1) * 128], index
-                    )
-                    picked = jnp.where(group == s, got, picked)
-                total = total - face_scale_ref[f : f + 1, span] * picked
-            n_ref[:, span] = total
-
-    minus_faces()
-    chosen = jnp.zeros((8, 512), F32)
-    for k in range(8):
-        chosen = jnp.where(child == k, n_ref[8 * k : 8 * k + 8, :], chosen)
-    high, low = halves(chosen)
-    both = jnp.concatenate([high, low], axis=0).astype(BF16)
-    summed = lax.dot_general(both, onehot_ref[...], NT, preferred_element_type=F32)
-    base_c = (summed[:8] + summed[8:]) * cinv
+    ghost_c = jnp.zeros((8, 128), F32)
+    for t in range(GROUPS):
+        span = slice(t * 128, (t + 1) * 128)
+        for f in range(FACES):
+            at = (f + 1) * 64 + 16 * t
+            row = child_ghost[f : f + 1, span]
+            even = from_ghosts(slice(at, at + 8), row)
+            odd = from_ghosts(slice(at + 8, at + 16), row)
+            ghost_c = ghost_c + child_weight[f : f + 1, span] * jnp.where(lane < 64, even, odd)
+    base_c = (local_c - (ghost_c + pltpu.roll(ghost_c, 64, 1))) * cinv
 
     def extend(parts, at):
         ext = parts[at]
@@ -543,7 +572,11 @@
                 pltpu.VMEM((64, 512), F32),
                 pltpu.VMEM((128, 512), F32),
                 pltpu.VMEM((56, 8, 128), F32),
-                pltpu.VMEM((128, 512), BF16),
+                pltpu.VMEM((64, 256), F32),
+                pltpu.VMEM((8, 256), jnp.int32),
+                pltpu.VMEM((8, 256), F32),
+                pltpu.VMEM((8, 512), jnp.int32),
+                pltpu.VMEM((8, 512), F32),
                 pltpu.VMEM((8, 512), jnp.int32),
                 pltpu.VMEM((4, 40, 128), F32),
                 pltpu.VMEM((4, 40, 128), F32),

time: 37 us -> 35.8 us (0.968)
  Pallas kernels: 34.3 us -> 33.1 us
    pallas_call x1, Pallas kernels: 34.3 us -> 33.1 us  [body(): pl.pallas_call(functools.partial(kernel, wide, narrow), out_shape=[pltpu....]
where the time goes in v3:
time: 35.8 us; the launch traced here: 35.7 us
  Pallas kernels  33.1 us (92%)
  between operations  1.29 us (4%)
  local copies, waits for them, and re-layouts  1.25 us (3%)
    pallas_call x1, Pallas kernels, body(): pl.pallas_call(functools.partial(kernel, wide, narrow), out_shape=[pltpu....  33.1 us
    unnamed x2, local copies, waits for them, and re-layouts  1.25 us

profile of v3, /device:TPU:1, one launch (start us, length us, event | category | flops | bytes accessed | tf_op | source)
XLA Modules:
  0.0 35.7 jit_solution(8095689539738822289)
XLA Ops:
  1.3 33.1 %shard_map.194 = (f32[64,512]{1,0:T(8,128)S(1)}, f32[8,64]{1,0:T(8,128)S(1)}) custom-call(f32[64,512]{1,0:T(8,128)} %start_hbm.1, f32[64,512]{1,0:T(8,128)} %right_hbm.1, f32[1,512]{1,0:T(1,128)} %bitcast.9, f32[6,512]{1,0:T(8,128)} %face_scale_hbm.1, s32[6,512]{1,0:T(8,128)} %nbr_hbm.1, s32[4,64]{1,0:T(4,128)} %send_hbm.1, s32[1,1]{1,0:T(1,128)} %bitcast.7.counts_hbm, ...), custom_call_target="tpu_custom_call" | custom-call | tf_op jit(solution)/shard_map/pallas_call | solution.py:551
  34.4 0.7 %copy.23 = f32[64,512]{1,0:T(8,128)} copy(f32[64,512]{1,0:T(8,128)S(1)} %get-tuple-element.2) | data formatting | bytes 262144
  35.1 0.6 %copy.24 = f32[8,64]{1,0:T(8,128)} copy(f32[8,64]{1,0:T(8,128)S(1)} %get-tuple-element.3) | data formatting | bytes 4096
